TPU v7x, 32 devices: a whole 2x2x4 slice. The times are simulated.
32 devices in a mesh: box: 4 (over y, x), dir: 8 (over z, core).
Axes of the slice: x: 2, y: 2, z: 4, core: 2. Of those that a mesh axis runs over, the one named last changes fastest.
Arguments:
- children: float32 [2, 512, 20480], P(None, 'box', 'dir'), may hold values from -6 to 6
- stencil_index: int32 [4, 81920], P(None, 'dir'), may hold values from 0 to 20479, as said below
- stencil_weights: float32 [4, 81920], P(None, 'dir'), may hold values from -0.25 to 1
- child_phase: float32 [8, 81920], P(None, 'dir'), may hold values from -3.140625 to 3.140625
- translations: float32 [2, 64, 4, 8, 2560], P(None, None, 'box'), may hold values from -0.4375 to 0.4375
- box_lengths: int32 [64], P('dir'), may hold values from 1 to 128, 3272 in all
- partner_ids: int32 [64, 128], P('dir'), may hold values from 0 to 63
- partner_kinds: int32 [64, 128], P('dir'), may hold values from 0 to 63
Outputs:
- incoming: float32 [2, 64, 4, 8, 2560], P(None, 'dir', 'box')
Inputs may be any that keep to these rules, and one draw needn't show every extreme that they name: stencil_index[s, m] lies within m // 4 - 2 to m // 4 + 3 taken modulo 20480, and both ends are reached. `box_lengths`: the lengths sum to 3272.
All inputs are finite; a program needn't handle non-finite values. No bound on the sum of `box_lengths` on one device may be relied on, other than what follows from the above.
Results may differ from a plain program's by a relative error of at most 0.0003.
Values sent between devices are 32-bit elements; how exact they have to be, the bound alone decides.
A program may use at most 128 MiB of HBM per device.

v0:
```python
import jax
import jax.numpy as jnp
from jax import lax
from jax.sharding import PartitionSpec as P

KA = 20480
HALO = 4


def extended_2(block, sides, width):
    for axis, dim in sides:
        count = lax.axis_size(axis)
        forward = [(i, i + 1) for i in range(count - 1)]
        forward.append((count - 1, 0))
        backward = [(target, source) for source, target in forward]
        low = lax.ppermute(
            lax.slice_in_dim(block, block.shape[dim] - width, None, axis=dim), axis, forward
        )
        high = lax.ppermute(lax.slice_in_dim(block, 0, width, axis=dim), axis, backward)
        block = jnp.concatenate([low, block, high], axis=dim)
    return block


def translate_boxes(sources, table, lengths, ids, kinds_index, count):
    list_slots = ids.shape[1]
    source_count = sources.shape[1]
    type_count = table.shape[1]
    slots = jnp.arange(list_slots, dtype=jnp.int32)
    source_range = jnp.arange(source_count, dtype=jnp.int32)
    type_range = jnp.arange(type_count, dtype=jnp.int32)

    def translate(target):
        live = (slots < lengths[target]).astype(jnp.float32)[:, None]
        source_hot = (ids[target][:, None] == source_range[None, :]).astype(jnp.float32) * live
        kind_hot = (kinds_index[target][:, None] == type_range[None, :]).astype(jnp.float32)
        counts = jnp.dot(kind_hot.T, source_hot, precision=lax.Precision.HIGHEST)
        summed = jnp.einsum("kj,cjr->ckr", counts, sources, precision=lax.Precision.HIGHEST)
        real_part = jnp.sum(table[0] * summed[0] - table[1] * summed[1], axis=0)
        imag_part = jnp.sum(table[0] * summed[1] + table[1] * summed[0], axis=0)
        return jnp.stack([real_part, imag_part])

    result = lax.map(translate, jnp.arange(count, dtype=jnp.int32))
    return jnp.transpose(result, (1, 0, 2))


def on_device(
    children,
    stencil_index,
    stencil_weights,
    child_phase,
    translations,
    box_lengths,
    partner_ids,
    partner_kinds,
):
    coarse_width = children.shape[2]
    fine_width = stencil_index.shape[1]
    ratio = fine_width // coarse_width
    extended = extended_2(children, (("dir", 2),), HALO)
    global_fine = lax.axis_index("dir") * fine_width + jnp.arange(fine_width, dtype=jnp.int32)
    centre = global_fine // 4
    offsets = (stencil_index - centre[None, :] + 2) % KA - 2
    child_rows = children.shape[1]
    fine = jnp.zeros((2, child_rows, fine_width), jnp.float32)
    for shift_by in range(-2, 4):
        weight_row = jnp.sum(stencil_weights * (offsets == shift_by).astype(jnp.float32), axis=0)
        slab = lax.slice_in_dim(extended, HALO + shift_by, HALO + shift_by + coarse_width, axis=2)
        widened = jnp.broadcast_to(
            slab[:, :, :, None], (2, child_rows, coarse_width, ratio)
        ).reshape(2, child_rows, fine_width)
        fine = fine + widened * weight_row[None, None, :]
    parents_here = child_rows // 8
    fine = fine.reshape(2, parents_here, 8, fine_width)
    cosine = jnp.cos(child_phase)
    sine = jnp.sin(child_phase)
    shifted_real = jnp.sum(fine[0] * cosine - fine[1] * sine, axis=1)
    shifted_imag = jnp.sum(fine[0] * sine + fine[1] * cosine, axis=1)
    outgoing = jnp.stack([shifted_real, shifted_imag])
    box_count = lax.axis_size("box")
    dir_count = lax.axis_size("dir")
    block_width = fine_width // box_count
    sectioned = outgoing.reshape(2, parents_here, box_count, 1, block_width)
    moved = lax.all_to_all(
        lax.all_to_all(sectioned, "box", split_axis=2, concat_axis=1, tiled=True),
        "dir",
        split_axis=1,
        concat_axis=3,
        tiled=True,
    )
    own_boxes = moved.shape[1]
    span = moved.shape[3] * moved.shape[4]
    radiated = moved.reshape(2, own_boxes, span)
    table = translations.reshape(2, translations.shape[1], span)
    sources = lax.all_gather(radiated, "dir", axis=1, tiled=True)
    result = translate_boxes(sources, table, box_lengths, partner_ids, partner_kinds, own_boxes)
    return result.reshape(2, own_boxes, 1, dir_count, span // dir_count)


def solution(mesh):
    return jax.shard_map(
        on_device,
        mesh=mesh,
        in_specs=(
            P(None, "box", "dir"),
            P(None, "dir"),
            P(None, "dir"),
            P(None, "dir"),
            P(None, None, "box", None, None),
            P("dir"),
            P("dir", None),
            P("dir", None),
        ),
        out_specs=P(None, "dir", "box", None, None),
        check_vma=False,
    )
```

profile of v0, /device:TPU:0, one launch (start us, length us, event | category | flops | bytes accessed | tf_op | source)
XLA Modules:
  0.0 451.8 jit_solution(5854241848503713584)
XLA Ops:
  44.6 6.8 %broadcast_in_dim.25 = f32[2,128,2560,4]{1,3,2,0:T(4,128)} broadcast(f32[2,128,2560]{1,2,0:T(8,128)} %copy.32), dimensions={0,1,2} | broadcast | bytes 13107200 | tf_op jit(solution)/shard_map/broadcast_in_dim | solution.py:68
  51.4 5.1 %broadcast_in_dim.26 = f32[2,128,2560,4]{1,3,2,0:T(4,128)} broadcast(f32[2,128,2560]{1,2,0:T(8,128)S(1)} %copy-done.3), dimensions={0,1,2} | broadcast | bytes 13107200 | tf_op jit(solution)/shard_map/broadcast_in_dim | solution.py:68
  56.5 5.1 %broadcast_in_dim.27 = f32[2,128,2560,4]{1,3,2,0:T(4,128)} broadcast(f32[2,128,2560]{1,2,0:T(8,128)S(1)} %copy-done.5), dimensions={0,1,2} | broadcast | bytes 13107200 | tf_op jit(solution)/shard_map/broadcast_in_dim | solution.py:68
  61.6 5.1 %broadcast_in_dim.22 = f32[2,128,2560,4]{1,3,2,0:T(4,128)} broadcast(f32[2,128,2560]{1,2,0:T(8,128)S(1)} %copy-done.4), dimensions={0,1,2} | broadcast | bytes 13107200 | tf_op jit(solution)/shard_map/broadcast_in_dim | solution.py:68
  66.6 5.1 %broadcast_in_dim.23 = f32[2,128,2560,4]{1,3,2,0:T(4,128)} broadcast(f32[2,128,2560]{1,2,0:T(8,128)S(1)} %copy-done.6), dimensions={0,1,2} | broadcast | bytes 13107200 | tf_op jit(solution)/shard_map/broadcast_in_dim | solution.py:68
  71.8 5.1 %broadcast_in_dim.24 = f32[2,128,2560,4]{1,3,2,0:T(4,128)} broadcast(f32[2,128,2560]{1,2,0:T(8,128)S(1)} %copy-done.1), dimensions={0,1,2} | broadcast | bytes 13107200 | tf_op jit(solution)/shard_map/broadcast_in_dim | solution.py:68
  76.9 24.1 %multiply_add_fusion = f32[2,128,10240]{1,2,0:T(8,128)} fusion(f32[2,128,10240]{1,2,0:T(8,128)} %bitcast.80, f32[2,128,10240]{1,2,0:T(8,128)} %bitcast.79, f32[2,128,10240]{1,2,0:T(8,128)} %bitcast.78, f32[2,128,10240]{1,2,0:T(8,128)} %bitcast.83, f32[2,128,10240]{1,2,0:T(8,128)} %bitcast.82, f32[2,128,10240]{1,2,0:T(8,128)} %bitcast.81, ...), kind=kLoop, calls=%fused_computation.21 | loop fusion | flops 28835840 | bytes 73646080 | tf_op jit(solution)/shard_map/add | solution.py:71
  100.9 7.3 %fusion.22 = (f32[1,128,10240]{1,2,0:T(8,128)}, f32[1,128,10240]{1,2,0:T(8,128)}) fusion(f32[2,128,10240]{1,2,0:T(8,128)} %multiply_add_fusion), kind=kLoop, calls=%fused_computation.55 | loop fusion | bytes 20971520 | tf_op jit(solution)/shard_map/slice | solution.py:76
  108.2 5.9 %copy.35 = f32[1,128,10240]{2,1,0:T(8,128)} copy(f32[1,128,10240]{1,2,0:T(8,128)} %get-tuple-element.158) | data formatting | bytes 10485760 | tf_op jit(solution)/shard_map/slice | solution.py:76
  114.1 6.0 %copy.36 = f32[1,128,10240]{2,1,0:T(8,128)} copy(f32[1,128,10240]{1,2,0:T(8,128)} %get-tuple-element.159) | data formatting | bytes 10485760 | tf_op jit(solution)/shard_map/slice | solution.py:76
  120.1 7.8 %fusion.14 = (f32[16,10240]{1,0:T(8,128)S(1)}, f32[16,10240]{1,0:T(8,128)S(1)}) fusion(f32[1,128,10240]{2,1,0:T(8,128)} %copy.36, f32[1,128,10240]{2,1,0:T(8,128)} %copy.35, f32[8,10240]{1,0:T(8,128)S(1)} %get-tuple-element.169, f32[8,10240]{1,0:T(8,128)S(1)} %get-tuple-element.168), kind=kLoop, calls=%fused_computation.25 | loop fusion | flops 10158080 | bytes 12451840 | tf_op jit(solution)/shard_map/reduce_sum | solution.py:76
  129.5 19.3 %all_to_all.33 = f32[2,16,4,1,2560]{4,1,3,0,2:T(8,128)S(1)} all-to-all(f32[2,16,4,1,2560]{4,1,3,0,2:T(8,128)S(1)} %copy.37), channel_id=1, replica_groups=mesh['box'=4,'dir'=8] {'box'}, dimensions={2} | all-to-all | bytes 2621440 | tf_op jit(solution)/shard_map/all_to_all | solution.py:84
  149.9 35.9 %all_to_all.34 = f32[2,64,1,1,2560]{4,0,3,2,1:T(2,128)S(1)} all-to-all(f32[2,64,1,1,2560]{4,0,3,2,1:T(2,128)S(1)} %copy.39), channel_id=1, replica_groups=mesh['box'=4,'dir'=8] {'dir'}, dimensions={1} | all-to-all | bytes 2621440 | tf_op jit(solution)/shard_map/all_to_all | solution.py:83
  187.1 10.9 %reshape.100 = f32[2,64,20480]{2,1,0:T(8,128)} reshape(f32[2,64,1,8,2560]{4,3,2,1,0:T(8,128)} %param.14) | data formatting | bytes 20971520 | tf_op jit(solution)/shard_map/reshape | solution.py:93
  198.0 86.0 %all-gather.2.cloned.1.call-done = f32[2,64,20480]{2,1,0:T(8,128)} async-done(((f32[2,8,20480]{2,1,0:T(8,128)}), f32[2,64,20480]{2,1,0:T(8,128)}) %all-gather.2.cloned.1.call-update) | async-done | bytes 10485776 | tf_op jit(solution)/shard_map/all_gather | solution.py:94
  284.1 158.6 %while.13 = (s32[]{:T(128)}, f32[8,2,20480]{2,1,0:T(2,128)S(1)}, f32[2,64,20480]{2,1,0:T(8,128)}, s32[8]{0:T(128)S(1)}, s32[8,128]{1,0:T(8,128)}, /*index=5*/s32...) while((s32[]{:T(128)}, f32[8,2,20480]{2,1,0:T(2,128)S(1)}, ...), condition=%wide.region_11.12_spmd.clone.clone, body=%wide.region_8.11_spmd.clone.clone.sunk | while | flops 2030067968 | bytes 73928960 | solution.py:42
  289.0 12.6 %convolution_bitcast_fusion.5 = f32[2,64,20480]{2,1,0:T(8,128)S(1)} fusion(f32[64,64,1]{1,0,2:T(8,128)S(1)} %convolution_bitcast_fusion.4, f32[2,64,20480]{2,1,0:T(8,128)} %get-tuple-element.256), kind=kOutput, calls=%fused_computation.2.clone.1 | convolution fusion | flops 2013265920 | bytes 20987904 | tf_op jit(solution)/shard_map/while/body/eval_jaxpr/kj,cjr->ckr/dot_general | solution.py:37
  308.8 12.6 %convolution_bitcast_fusion.5 = f32[2,64,20480]{2,1,0:T(8,128)S(1)} fusion(f32[64,64,1]{1,0,2:T(8,128)S(1)} %convolution_bitcast_fusion.4, f32[2,64,20480]{2,1,0:T(8,128)} %get-tuple-element.256), kind=kOutput, calls=%fused_computation.2.clone.1 | convolution fusion | flops 2013265920 | bytes 20987904 | tf_op jit(solution)/shard_map/while/body/eval_jaxpr/kj,cjr->ckr/dot_general | solution.py:37
  328.7 12.6 %convolution_bitcast_fusion.5 = f32[2,64,20480]{2,1,0:T(8,128)S(1)} fusion(f32[64,64,1]{1,0,2:T(8,128)S(1)} %convolution_bitcast_fusion.4, f32[2,64,20480]{2,1,0:T(8,128)} %get-tuple-element.256), kind=kOutput, calls=%fused_computation.2.clone.1 | convolution fusion | flops 2013265920 | bytes 20987904 | tf_op jit(solution)/shard_map/while/body/eval_jaxpr/kj,cjr->ckr/dot_general | solution.py:37
  348.5 12.6 %convolution_bitcast_fusion.5 = f32[2,64,20480]{2,1,0:T(8,128)S(1)} fusion(f32[64,64,1]{1,0,2:T(8,128)S(1)} %convolution_bitcast_fusion.4, f32[2,64,20480]{2,1,0:T(8,128)} %get-tuple-element.256), kind=kOutput, calls=%fused_computation.2.clone.1 | convolution fusion | flops 2013265920 | bytes 20987904 | tf_op jit(solution)/shard_map/while/body/eval_jaxpr/kj,cjr->ckr/dot_general | solution.py:37
  368.3 12.6 %convolution_bitcast_fusion.5 = f32[2,64,20480]{2,1,0:T(8,128)S(1)} fusion(f32[64,64,1]{1,0,2:T(8,128)S(1)} %convolution_bitcast_fusion.4, f32[2,64,20480]{2,1,0:T(8,128)} %get-tuple-element.256), kind=kOutput, calls=%fused_computation.2.clone.1 | convolution fusion | flops 2013265920 | bytes 20987904 | tf_op jit(solution)/shard_map/while/body/eval_jaxpr/kj,cjr->ckr/dot_general | solution.py:37
  388.1 12.6 %convolution_bitcast_fusion.5 = f32[2,64,20480]{2,1,0:T(8,128)S(1)} fusion(f32[64,64,1]{1,0,2:T(8,128)S(1)} %convolution_bitcast_fusion.4, f32[2,64,20480]{2,1,0:T(8,128)} %get-tuple-element.256), kind=kOutput, calls=%fused_computation.2.clone.1 | convolution fusion | flops 2013265920 | bytes 20987904 | tf_op jit(solution)/shard_map/while/body/eval_jaxpr/kj,cjr->ckr/dot_general | solution.py:37
  408.0 12.6 %convolution_bitcast_fusion.5 = f32[2,64,20480]{2,1,0:T(8,128)S(1)} fusion(f32[64,64,1]{1,0,2:T(8,128)S(1)} %convolution_bitcast_fusion.4, f32[2,64,20480]{2,1,0:T(8,128)} %get-tuple-element.256), kind=kOutput, calls=%fused_computation.2.clone.1 | convolution fusion | flops 2013265920 | bytes 20987904 | tf_op jit(solution)/shard_map/while/body/eval_jaxpr/kj,cjr->ckr/dot_general | solution.py:37
  427.8 12.6 %convolution_bitcast_fusion.5 = f32[2,64,20480]{2,1,0:T(8,128)S(1)} fusion(f32[64,64,1]{1,0,2:T(8,128)S(1)} %convolution_bitcast_fusion.4, f32[2,64,20480]{2,1,0:T(8,128)} %get-tuple-element.256), kind=kOutput, calls=%fused_computation.2.clone.1 | convolution fusion | flops 2013265920 | bytes 20987904 | tf_op jit(solution)/shard_map/while/body/eval_jaxpr/kj,cjr->ckr/dot_general | solution.py:37
  (158 shorter events, 84.5 us)
Async XLA Ops:
  6.5 13.7 %copy-start = (f32[2,128,2560]{2,1,0:T(8,128)S(1)}, f32[2,128,2560]{2,1,0:T(8,128)}, u32[]{:S(2)}) copy-start(f32[2,128,2560]{2,1,0:T(8,128)} %param.10) | copy-start | bytes 7864324
  6.5 277.5 %all-gather.2.cloned.1.call-start = ((), (), s32[]{:S(2)}) async-start(), calls=%async_computation.2 | async-start | bytes 11796480 | tf_op jit(solution)/shard_map/all_gather | solution.py:94
  8.4 11.8 %collective-permute-start = (f32[2,128,4]{2,1,0:T(8,128)}, f32[2,128,4]{2,1,0:T(8,128)}, u32[]{:S(2)}, u32[]{:S(2)}) collective-permute-start(f32[2,128,4]{2,1,0:T(8,128)} %get-tuple-element.166), channel_id=1, source_target_pairs={{0,1},{1,2},{2,3},{3,4},{4,5},{5,6},{6,7},{7,0},{8,9},{9,10},{10,1... | collective-permute-start | bytes 12296 | tf_op jit(solution)/shard_map/ppermute | solution.py:16
  8.9 16.3 %collective-permute-start.1 = (f32[2,128,4]{2,1,0:T(8,128)}, f32[2,128,4]{2,1,0:T(8,128)}, u32[]{:S(2)}, u32[]{:S(2)}) collective-permute-start(f32[2,128,4]{2,1,0:T(8,128)} %get-tuple-element.167), channel_id=1, source_target_pairs={{1,0},{2,1},{3,2},{4,3},{5,4},{6,5},{7,6},{0,7},{9,8},{10,9},{11,1... | collective-permute-start | bytes 12296 | tf_op jit(solution)/shard_map/ppermute | solution.py:19
  187.1 96.9 %copy-start.7 = (s32[8]{0:T(128)S(1)}, s32[8]{0:T(128)}, u32[]{:S(2)}) copy-start(s32[8]{0:T(128)} %param.15) | copy-start | bytes 100
  284.6 17.0 %slice-start = ((s8[10485760]{0:T(1024)(128)(4,1)}), s8[2097152]{0:T(1024)(128)(4,1)S(1)}, s32[]{:S(2)}) async-start(s8[10485760]{0:T(1024)(128)(4,1)} %bitcast.76), calls=%async_computation.3 | async-start | bytes 4194304 | tf_op jit(solution)/shard_map/while
  304.5 17.0 %slice-start = ((s8[10485760]{0:T(1024)(128)(4,1)}), s8[2097152]{0:T(1024)(128)(4,1)S(1)}, s32[]{:S(2)}) async-start(s8[10485760]{0:T(1024)(128)(4,1)} %bitcast.76), calls=%async_computation.3 | async-start | bytes 4194304 | tf_op jit(solution)/shard_map/while
  308.8 12.7 %slice-start.1 = ((s8[10485760]{0:T(1024)(128)(4,1)}), s8[4194304]{0:T(1024)(128)(4,1)S(1)}, s32[]{:S(2)}) async-start(s8[10485760]{0:T(1024)(128)(4,1)} %bitcast.76), calls=%async_computation.4 | async-start | bytes 8388608 | tf_op jit(solution)/shard_map/while
  308.8 12.7 %slice-start.2 = ((s8[10485760]{0:T(1024)(128)(4,1)}), s8[4194304]{0:T(1024)(128)(4,1)S(1)}, s32[]{:S(2)}) async-start(s8[10485760]{0:T(1024)(128)(4,1)} %bitcast.76), calls=%async_computation.5 | async-start | bytes 8388608 | tf_op jit(solution)/shard_map/while
  324.3 17.0 %slice-start = ((s8[10485760]{0:T(1024)(128)(4,1)}), s8[2097152]{0:T(1024)(128)(4,1)S(1)}, s32[]{:S(2)}) async-start(s8[10485760]{0:T(1024)(128)(4,1)} %bitcast.76), calls=%async_computation.3 | async-start | bytes 4194304 | tf_op jit(solution)/shard_map/while
  328.6 12.7 %slice-start.1 = ((s8[10485760]{0:T(1024)(128)(4,1)}), s8[4194304]{0:T(1024)(128)(4,1)S(1)}, s32[]{:S(2)}) async-start(s8[10485760]{0:T(1024)(128)(4,1)} %bitcast.76), calls=%async_computation.4 | async-start | bytes 8388608 | tf_op jit(solution)/shard_map/while
  328.6 12.7 %slice-start.2 = ((s8[10485760]{0:T(1024)(128)(4,1)}), s8[4194304]{0:T(1024)(128)(4,1)S(1)}, s32[]{:S(2)}) async-start(s8[10485760]{0:T(1024)(128)(4,1)} %bitcast.76), calls=%async_computation.5 | async-start | bytes 8388608 | tf_op jit(solution)/shard_map/while
  344.1 17.0 %slice-start = ((s8[10485760]{0:T(1024)(128)(4,1)}), s8[2097152]{0:T(1024)(128)(4,1)S(1)}, s32[]{:S(2)}) async-start(s8[10485760]{0:T(1024)(128)(4,1)} %bitcast.76), calls=%async_computation.3 | async-start | bytes 4194304 | tf_op jit(solution)/shard_map/while
  348.5 12.7 %slice-start.1 = ((s8[10485760]{0:T(1024)(128)(4,1)}), s8[4194304]{0:T(1024)(128)(4,1)S(1)}, s32[]{:S(2)}) async-start(s8[10485760]{0:T(1024)(128)(4,1)} %bitcast.76), calls=%async_computation.4 | async-start | bytes 8388608 | tf_op jit(solution)/shard_map/while
  348.5 12.7 %slice-start.2 = ((s8[10485760]{0:T(1024)(128)(4,1)}), s8[4194304]{0:T(1024)(128)(4,1)S(1)}, s32[]{:S(2)}) async-start(s8[10485760]{0:T(1024)(128)(4,1)} %bitcast.76), calls=%async_computation.5 | async-start | bytes 8388608 | tf_op jit(solution)/shard_map/while
  363.9 17.0 %slice-start = ((s8[10485760]{0:T(1024)(128)(4,1)}), s8[2097152]{0:T(1024)(128)(4,1)S(1)}, s32[]{:S(2)}) async-start(s8[10485760]{0:T(1024)(128)(4,1)} %bitcast.76), calls=%async_computation.3 | async-start | bytes 4194304 | tf_op jit(solution)/shard_map/while
  368.3 12.7 %slice-start.1 = ((s8[10485760]{0:T(1024)(128)(4,1)}), s8[4194304]{0:T(1024)(128)(4,1)S(1)}, s32[]{:S(2)}) async-start(s8[10485760]{0:T(1024)(128)(4,1)} %bitcast.76), calls=%async_computation.4 | async-start | bytes 8388608 | tf_op jit(solution)/shard_map/while
  368.3 12.7 %slice-start.2 = ((s8[10485760]{0:T(1024)(128)(4,1)}), s8[4194304]{0:T(1024)(128)(4,1)S(1)}, s32[]{:S(2)}) async-start(s8[10485760]{0:T(1024)(128)(4,1)} %bitcast.76), calls=%async_computation.5 | async-start | bytes 8388608 | tf_op jit(solution)/shard_map/while
  383.8 17.0 %slice-start = ((s8[10485760]{0:T(1024)(128)(4,1)}), s8[2097152]{0:T(1024)(128)(4,1)S(1)}, s32[]{:S(2)}) async-start(s8[10485760]{0:T(1024)(128)(4,1)} %bitcast.76), calls=%async_computation.3 | async-start | bytes 4194304 | tf_op jit(solution)/shard_map/while
  388.1 12.7 %slice-start.1 = ((s8[10485760]{0:T(1024)(128)(4,1)}), s8[4194304]{0:T(1024)(128)(4,1)S(1)}, s32[]{:S(2)}) async-start(s8[10485760]{0:T(1024)(128)(4,1)} %bitcast.76), calls=%async_computation.4 | async-start | bytes 8388608 | tf_op jit(solution)/shard_map/while
  403.6 17.0 %slice-start = ((s8[10485760]{0:T(1024)(128)(4,1)}), s8[2097152]{0:T(1024)(128)(4,1)S(1)}, s32[]{:S(2)}) async-start(s8[10485760]{0:T(1024)(128)(4,1)} %bitcast.76), calls=%async_computation.3 | async-start | bytes 4194304 | tf_op jit(solution)/shard_map/while
  407.9 12.7 %slice-start.1 = ((s8[10485760]{0:T(1024)(128)(4,1)}), s8[4194304]{0:T(1024)(128)(4,1)S(1)}, s32[]{:S(2)}) async-start(s8[10485760]{0:T(1024)(128)(4,1)} %bitcast.76), calls=%async_computation.4 | async-start | bytes 8388608 | tf_op jit(solution)/shard_map/while
  423.4 17.0 %slice-start = ((s8[10485760]{0:T(1024)(128)(4,1)}), s8[2097152]{0:T(1024)(128)(4,1)S(1)}, s32[]{:S(2)}) async-start(s8[10485760]{0:T(1024)(128)(4,1)} %bitcast.76), calls=%async_computation.3 | async-start | bytes 4194304 | tf_op jit(solution)/shard_map/while
  427.8 12.7 %slice-start.1 = ((s8[10485760]{0:T(1024)(128)(4,1)}), s8[4194304]{0:T(1024)(128)(4,1)S(1)}, s32[]{:S(2)}) async-start(s8[10485760]{0:T(1024)(128)(4,1)} %bitcast.76), calls=%async_computation.4 | async-start | bytes 8388608 | tf_op jit(solution)/shard_map/while
  (11 other events, 97.0 us)
Sparse Core Ops, SparseCore 0:
  187.2 96.7 all-gather.1
where the time goes:
time: 453 us; the launch traced here: 452 us
  local copies, waits for them, and re-layouts  110 us (24%)
  matrix products  103 us (23%)
  waiting for transfers between devices  86 us (19%)
  other arithmetic  61.8 us (14%)
  blocking collectives  55.2 us (12%)
  loops' own time  17.5 us (4%)
  between operations  13.5 us (3%)
    dot_general x8, matrix products, translate(): jnp.einsum('kj,cjr->ckr', counts, sources, precision=lax.Precision.HIGHEST)  101 us
    all_gather x1, waiting for transfers between devices, on_device(): sources = lax.all_gather(radiated, 'dir', axis=1, tiled=True)  86 us
    all_to_all x1, blocking collectives, on_device(): lax.all_to_all(lax.all_to_all(sectioned, 'box', split_axis=2, concat_axis...  35.9 us
    broadcast_in_dim x6, local copies, waits for them, and re-layouts, on_device(): jnp.broadcast_to(slab[:, :, :, None], (2, child_rows, coarse_width, ratio))  32.2 us
    add x1, other arithmetic, on_device(): fine = fine + widened * weight_row[None, None, :]  24.1 us
    all_to_all x1, blocking collectives, on_device(): lax.all_to_all(sectioned, 'box', split_axis=2, concat_axis=1, tiled=True)  19.3 us
    slice x3, local copies, waits for them, and re-layouts, on_device(): shifted_real = jnp.sum(fine[0] * cosine - fine[1] * sine, axis=1)  19.1 us
    slice x6, local copies, waits for them, and re-layouts, on_device(): lax.slice_in_dim(extended, HALO + shift_by, HALO + shift_by + coarse_widt...  18.5 us
  transfers between devices with their start and end apart: 3, of which 1 were waited for; matrix products, arithmetic and copies ran while one was open for 5% of the time, Pallas kernels for 0%

commit v1 on v0

v1 whole, which is shorter than its diff:
```python
import functools

import jax
import jax.numpy as jnp
from jax import lax
from jax.experimental import pallas as pl
from jax.experimental.pallas import tpu as pltpu
from jax.sharding import PartitionSpec as P

LANES = 128
F32 = jnp.float32
BF16 = jnp.bfloat16
SIN_TERMS = (1.0, -1 / 6, 1 / 120, -1 / 5040, 1 / 362880, -1 / 39916800, 1 / 6227020800)
COS_TERMS = (1.0, -1 / 2, 1 / 24, -1 / 720, 1 / 40320, -1 / 3628800, 1 / 479001600)


def split(value):
    high = value.astype(BF16)
    return high, (value - high.astype(F32)).astype(BF16)


def series(terms, square):
    total = jnp.full_like(square, terms[-1])
    for term in terms[-2::-1]:
        total = total * square + term
    return total


def sine_cosine(angle):
    half = angle * 0.5
    square = half * half
    sine = half * series(SIN_TERMS, square)
    cosine = series(COS_TERMS, square)
    return 2.0 * sine * cosine, 1.0 - 2.0 * sine * sine


def shifted_tile(before, tile):
    lane = lax.broadcasted_iota(jnp.int32, tile.shape, 1)
    return jnp.where(lane < 2, pltpu.roll(before, 2, axis=1), pltpu.roll(tile, 2, axis=1))


def rows_of(ref, part, octant, parents):
    return ref[part, pl.ds(octant, parents, stride=8), :]


def prepare_columns(held_ref, left_ref, right_ref, tile, high_ref, low_ref, parents):
    tiles = held_ref.shape[0]
    edge = isinstance(tile, int)
    here = right_ref if edge and tile == tiles else held_ref.at[tile]
    before = left_ref if edge and tile == 0 else held_ref.at[tile - 1]
    column = tile * LANES if edge else pl.multiple_of(tile * LANES, LANES)
    for octant in range(8):
        for part in range(2):
            moved = shifted_tile(
                rows_of(before, part, octant, parents), rows_of(here, part, octant, parents)
            )
            high, low = split(moved)
            rows = pl.ds((octant * 2 + part) * parents, parents)
            high_ref[rows, pl.ds(column, LANES)] = high
            low_ref[rows, pl.ds(column, LANES)] = low


def block_layout(width, span):
    block = 512 if span % 512 == 0 else span
    return block, (256 if block == 512 else -(-(block // 4 + 128) // LANES) * LANES)


def band_matrix(index_ref, weight_ref, start, first, shift, block, total, high_ref, low_ref):
    lane = lax.broadcasted_iota(jnp.int32, (1, LANES), 1) // 4
    row = lax.broadcasted_iota(jnp.int32, (48, LANES), 0)
    for tile in range(block // LANES):
        column = pl.multiple_of(start + tile * LANES, LANES)
        centre = (first + start + tile * LANES) // 4 + lane
        band = jnp.zeros((48, LANES), F32)
        for point in range(index_ref.shape[0]):
            offset = index_ref[pl.ds(point, 1), pl.ds(column, LANES)] - centre + 2
            offset = jnp.where(offset < 0, offset + total, offset)
            offset = jnp.where(offset >= total, offset - total, offset) + lane
            band = band + jnp.where(row == offset, weight_ref[pl.ds(point, 1), pl.ds(column, LANES)], 0.0)
        high, low = split(band)
        rows = pl.ds(shift + tile * 32, 48)
        high_ref[rows, pl.ds(tile * LANES, LANES)] = high
        low_ref[rows, pl.ds(tile * LANES, LANES)] = low


def aggregate_block(refs, start, base, shift, first, block, total, parents, store):
    index_ref, weight_ref, phase_ref, high_ref, low_ref, band_high, band_low, fine_ref = refs
    depth = band_high.shape[0]
    band_matrix(index_ref, weight_ref, start, first, shift, block, total, band_high, band_low)
    window = pl.ds(base, depth)
    lhs = jnp.concatenate([high_ref[:, window], high_ref[:, window], low_ref[:, window]], axis=1)
    rhs = jnp.concatenate([band_high[...], band_low[...], band_high[...]], axis=0)
    fine_ref[...] = jnp.dot(lhs, rhs, preferred_element_type=F32)
    for tile in range(block // LANES):
        lanes = pl.ds(tile * LANES, LANES)
        sine, cosine = sine_cosine(phase_ref[:, pl.ds(pl.multiple_of(start + tile * LANES, LANES), LANES)])
        real = jnp.zeros((parents, LANES), F32)
        imag = jnp.zeros((parents, LANES), F32)
        for octant in range(8):
            s, c = sine[octant : octant + 1], cosine[octant : octant + 1]
            fine_real = fine_ref[pl.ds(octant * 2 * parents, parents), lanes]
            fine_imag = fine_ref[pl.ds((octant * 2 + 1) * parents, parents), lanes]
            real = real + (fine_real * c - fine_imag * s)
            imag = imag + (fine_real * s + fine_imag * c)
        store(tile, real, imag)


def aggregate_kernel(
    parents, span, total, children_ref, left_ref, right_ref, index_ref, weight_ref, phase_ref, out_ref,
    held_ref, high_ref, low_ref, band_high, band_low, fine_ref, load_sems,
):
    fine = index_ref.shape[1]
    block = fine_ref.shape[1]
    first = lax.axis_index("dir") * fine
    tiles = held_ref.shape[0]
    loads = [
        pltpu.make_async_copy(
            children_ref.at[:, :, pl.ds(tile * LANES, LANES)], held_ref.at[tile], load_sems.at[tile]
        )
        for tile in range(tiles)
    ]
    for load in loads:
        load.start()
    for load in loads:
        load.wait()

    @pl.loop(1, tiles)
    def _(tile):
        prepare_columns(held_ref, left_ref, right_ref, tile, high_ref, low_ref, parents)

    prepare_columns(held_ref, left_ref, right_ref, 0, high_ref, low_ref, parents)
    prepare_columns(held_ref, left_ref, right_ref, tiles, high_ref, low_ref, parents)
    refs = (index_ref, weight_ref, phase_ref, high_ref, low_ref, band_high, band_low, fine_ref)
    per_section = span // block

    def clear():
        band_high[...] = jnp.zeros_like(band_high)
        band_low[...] = jnp.zeros_like(band_low)

    def run(start, base, shift, section, column):
        def store(tile, real, imag):
            lanes = pl.ds(pl.multiple_of(column + tile * LANES, LANES), LANES)
            out_ref[section, 0, :, lanes] = real
            out_ref[section, 1, :, lanes] = imag

        aggregate_block(refs, start, base, shift, first, block, total, parents, store)

    if block == 512:
        clear()

        @pl.loop(0, fine // block)
        def _(i):
            run(
                pl.multiple_of(i * block, block), pl.multiple_of(i * LANES, LANES), 0,
                i // per_section, pl.multiple_of((i % per_section) * block, block),
            )
    else:
        for i in range(fine // block):
            clear()
            coarse = i * block // 4
            base = coarse // LANES * LANES
            run(i * block, base, coarse - base, i // per_section, (i % per_section) * block)


def count_pairs(ids_ref, kinds_ref, lengths_ref, kinds, sources, loose_ref, counts_ref):
    slots = ids_ref.shape[1]
    slot = lax.broadcasted_iota(jnp.int32, (1, slots), 1)
    kind = lax.broadcasted_iota(jnp.int32, (kinds, slots), 0)
    source = lax.broadcasted_iota(jnp.int32, (2 * sources, slots), 0) % sources

    @pl.loop(0, counts_ref.shape[0])
    def _(d):
        for p in range(8):
            at = pl.ds(d * 8 + p, 1)
            live = slot < lengths_ref[at, :]
            kind_hot = ((kind == kinds_ref[at, :]) & live).astype(F32).astype(BF16)
            source_hot = (source == ids_ref[at, :]).astype(F32).astype(BF16)
            pairs = lax.dot_general(
                kind_hot, source_hot, (((1,), (1,)), ((), ())), preferred_element_type=F32
            )
            for part in range(loose_ref.shape[0]):
                loose_ref[part, pl.ds(p, kinds, stride=8), :] = pairs[:, part * LANES : (part + 1) * LANES]
        for part in range(loose_ref.shape[0]):
            counts_ref[d, :, pl.ds(part * LANES, LANES)] = loose_ref[part].astype(BF16)


def load_sources(grid_ref, column, tiles, sources_ref):
    blocks, _, parents, _ = grid_ref.shape
    sources = blocks * parents
    for tile in range(tiles):
        lanes = pl.ds(pl.multiple_of(column + tile * LANES, LANES), LANES)
        for b in range(blocks):
            for part in range(2):
                high, low = split(grid_ref[b, part, :, lanes])
                columns = pl.ds(part * LANES, LANES)
                sources_ref[tile, pl.ds(b * parents, parents), columns] = high
                sources_ref[tile, pl.ds(sources + b * parents, parents), columns] = low


def translate_tile(counts_ref, sources_ref, table_ref, d, tile, column, kinds):
    summed = jnp.dot(counts_ref[d], sources_ref[tile], preferred_element_type=F32)
    lanes = pl.ds(column, LANES)
    real = jnp.zeros((8, LANES), F32)
    imag = jnp.zeros((8, LANES), F32)
    for k in range(kinds):
        table_real = table_ref[0, pl.ds(k, 1), lanes]
        table_imag = table_ref[1, pl.ds(k, 1), lanes]
        summed_real = summed[k * 8 : k * 8 + 8, :LANES]
        summed_imag = summed[k * 8 : k * 8 + 8, LANES:]
        real = real + (table_real * summed_real - table_imag * summed_imag)
        imag = imag + (table_real * summed_imag + table_imag * summed_real)
    return real, imag


def translate_kernel(
    grid_ref, table_ref, ids_ref, kinds_ref, lengths_ref, out_ref, loose_ref, counts_ref, sources_ref
):
    kinds = table_ref.shape[1]
    count_pairs(ids_ref, kinds_ref, lengths_ref, kinds, sources_ref.shape[1] // 2, loose_ref, counts_ref)
    tiles = sources_ref.shape[0]
    load_sources(grid_ref, 0, tiles, sources_ref)

    @pl.loop(0, tiles)
    def _(tile):
        column = pl.multiple_of(tile * LANES, LANES)

        @pl.loop(0, out_ref.shape[0])
        def _(d):
            real, imag = translate_tile(counts_ref, sources_ref, table_ref, d, tile, column, kinds)
            out_ref[d, 0, :, pl.ds(column, LANES)] = real
            out_ref[d, 1, :, pl.ds(column, LANES)] = imag


def on_device(
    children, stencil_index, stencil_weights, child_phase, translations, box_lengths, partner_ids, partner_kinds
):
    box_count = lax.axis_size("box")
    dir_count = lax.axis_size("dir")
    rows, coarse = children.shape[1:]
    fine = stencil_index.shape[1]
    parents = rows // 8
    span = fine // box_count
    kinds = translations.shape[1]
    sources = parents * box_count
    block, depth = block_layout(fine, span)
    forward = [(i, (i + 1) % dir_count) for i in range(dir_count)]
    backward = [(b, a) for a, b in forward]
    left = lax.ppermute(children[:, :, coarse - LANES :], "dir", forward)
    right = lax.ppermute(children[:, :, :LANES], "dir", backward)
    lengths = jnp.broadcast_to(box_lengths[:, None], partner_ids.shape)
    lists = lax.all_gather(jnp.stack([partner_ids, partner_kinds, lengths]), "dir", axis=1, tiled=True)
    outgoing = pl.pallas_call(
        functools.partial(aggregate_kernel, parents, span, coarse * dir_count),
        out_shape=jax.ShapeDtypeStruct((box_count, 2, parents, span), F32),
        in_specs=[pl.BlockSpec(memory_space=pl.ANY)] + [pl.BlockSpec(memory_space=pltpu.VMEM)] * 5,
        scratch_shapes=[
            pltpu.VMEM((coarse // LANES, 2, rows, LANES), F32),
            pltpu.VMEM((2 * rows, coarse + LANES), BF16),
            pltpu.VMEM((2 * rows, coarse + LANES), BF16),
            pltpu.VMEM((depth, block), BF16),
            pltpu.VMEM((depth, block), BF16),
            pltpu.VMEM((2 * rows, block), F32),
            pltpu.SemaphoreType.DMA((coarse // LANES,)),
        ],
        compiler_params=pltpu.CompilerParams(vmem_limit_bytes=48 << 20),
    )(children, left, right, stencil_index, stencil_weights, child_phase)
    grid = lax.all_to_all(outgoing, "box", split_axis=0, concat_axis=0, tiled=True)
    table = lax.dynamic_index_in_dim(translations[:, :, 0], lax.axis_index("dir"), axis=2, keepdims=False)
    result = pl.pallas_call(
        translate_kernel,
        out_shape=jax.ShapeDtypeStruct((dir_count, 2, 8, span), F32),
        scratch_shapes=[
            pltpu.VMEM((2 * sources // LANES, kinds * 8, LANES), F32),
            pltpu.VMEM((dir_count, kinds * 8, 2 * sources), BF16),
            pltpu.VMEM((span // LANES, 2 * sources, 2 * LANES), BF16),
        ],
        compiler_params=pltpu.CompilerParams(vmem_limit_bytes=48 << 20),
    )(grid, table, lists[0], lists[1], lists[2])
    result = lax.all_to_all(result, "dir", split_axis=0, concat_axis=0, tiled=True)
    return jnp.transpose(result, (1, 2, 0, 3))[:, :, None]


def solution(mesh):
    return jax.shard_map(
        on_device,
        mesh=mesh,
        in_specs=(
            P(None, "box", "dir"),
            P(None, "dir"),
            P(None, "dir"),
            P(None, "dir"),
            P(None, None, "box", None, None),
            P("dir"),
            P("dir", None),
            P("dir", None),
        ),
        out_specs=P(None, "dir", "box", None, None),
        check_vma=False,
    )
```

time: 453 us -> 133 us (0.29)
  matrix products: 103 us -> 0 us
  local copies, waits for them, and re-layouts: 110 us -> 13.2 us
  waiting for transfers between devices: 86 us -> 6.19 us
  other arithmetic: 61.8 us -> 0.01 us
  Pallas kernels: 0 us -> 56.4 us
  loops' own time: 17.5 us -> 0 us
  between operations: 13.5 us -> 0.07 us
  blocking collectives: 55.2 us -> 48.6 us
    dot_general x16 -> x0, matrix products: 103 us -> none  [the longest x8 101 us: translate(): jnp.einsum('kj,cjr->ckr', counts, sources, precision=lax.Precision.HIGHEST)]
    all_gather x1 -> x0, waiting for transfers between devices: 86 us -> none  [on_device(): sources = lax.all_gather(radiated, 'dir', axis=1, tiled=True)]
    pallas_call x0 -> x2, Pallas kernels: none -> 56.4 us  [the longest x1 42.8 us: on_device(): pl.pallas_call(translate_kernel, out_shape=jax.ShapeDtypeStruct((dir_coun...]
    slice x10 -> x1, local copies, waits for them, and re-layouts: 39.5 us -> 0.99 us  [on_device(): right = lax.ppermute(children[:, :, :LANES], 'dir', backward)]
    broadcast_in_dim x6 -> x1, local copies, waits for them, and re-layouts: 32.2 us -> 1.82 us  [on_device(): return jnp.transpose(result, (1, 2, 0, 3))[:, :, None]]
    reduce_sum x10 -> x0, other arithmetic: 25.8 us -> none  [the longest x8 16.1 us: translate(): real_part = jnp.sum(table[0] * summed[0] - table[1] * summed[1], axis=0)]
    add x1 -> x0, other arithmetic: 24.1 us -> none  [on_device(): fine = fine + widened * weight_row[None, None, :]]
    all_to_all x2 -> x1, blocking collectives: 55.2 us -> 34.6 us  [on_device(): lax.all_to_all(result, 'dir', split_axis=0, concat_axis=0, tiled=True)]
  transfers between devices with their start and end apart: 3 -> 3, of which waited for: 1 -> 2; matrix products, arithmetic and copies ran while one was open for 5% -> 4% of each run, Pallas kernels for 0% -> 0%
where the time goes in v1:
time: 133 us
  Pallas kernels  56.4 us (42%)
  blocking collectives  48.6 us (37%)
  local copies, waits for them, and re-layouts  13.2 us (10%)
  starting transfers between devices  8.28 us (6%)
  waiting for transfers between devices  6.19 us (5%)
    pallas_call x1, Pallas kernels, on_device(): pl.pallas_call(translate_kernel, out_shape=jax.ShapeDtypeStruct((dir_coun...  42.8 us
    all_to_all x1, blocking collectives, on_device(): lax.all_to_all(result, 'dir', split_axis=0, concat_axis=0, tiled=True)  34.6 us
    all_gather x1, blocking collectives, on_device(): lax.all_gather(jnp.stack([partner_ids, partner_kinds, lengths]), 'dir', a...  13.9 us
    pallas_call x1, Pallas kernels, on_device(): pl.pallas_call(functools.partial(aggregate_kernel, parents, span, coarse...  13.6 us
    unnamed x15, local copies, waits for them, and re-layouts  5.17 us
    dynamic_slice x1, local copies, waits for them, and re-layouts, on_device(): lax.dynamic_index_in_dim(translations[:, :, 0], lax.axis_index('dir'), ax...  5.17 us
    ppermute x1, starting transfers between devices, on_device(): right = lax.ppermute(children[:, :, :LANES], 'dir', backward)  4.54 us
    all_to_all x1, starting transfers between devices, on_device(): lax.all_to_all(outgoing, 'box', split_axis=0, concat_axis=0, tiled=True)  3.73 us
  transfers between devices with their start and end apart: 3, of which 2 were waited for; matrix products, arithmetic and copies ran while one was open for 4% of the time, Pallas kernels for 0%

profile of v1, /device:TPU:0, one launch (start us, length us, event | category | flops | bytes accessed | tf_op | source)
XLA Modules:
  0.0 132.8 jit_solution(16894442406827105260)
XLA Ops:
  0.0 1.0 fusion
  1.0 4.5 %collective-permute-start.1 = (f32[2,128,128]{2,1,0:T(8,128)S(1)}, f32[2,128,128]{2,1,0:T(8,128)S(1)}, u32[]{:S(2)}, u32[]{:S(2)}) collective-permute-start(f32[2,128,128]{2,1,0:T(8,128)S(1)} %get-tuple-element.5), channel_id=1, source_target_pairs={{1,0},{2,1},{3,2},{4,3},{5,4},{6,5},{7,6},{0,7},{9,8},{10,9},{11,1... | collective-permute-start | bytes 393224 | tf_op jit(solution)/shard_map/ppermute | solution.py:249
  5.5 0.0 collective-permute-start
  5.5 2.5 %collective-permute-done.1.right_ref = f32[2,128,128]{2,1,0:T(8,128)S(1)} collective-permute-done((f32[2,128,128]{2,1,0:T(8,128)S(1)}, f32[2,128,128]{2,1,0:T(8,128)S(1)}, u32[]{:S(2)}, u32[]{:S(2)}) %collective-permute-start.1) | collective-permute-done | bytes 131104 | tf_op jit(solution)/shard_map/ppermute | solution.py:249
  8.1 3.7 %collective-permute-done.left_ref = f32[2,128,128]{2,1,0:T(8,128)S(1)} collective-permute-done((f32[2,128,128]{2,1,0:T(8,128)S(1)}, f32[2,128,128]{2,1,0:T(8,128)S(1)}, u32[]{:S(2)}, u32[]{:S(2)}) %collective-permute-start) | collective-permute-done | bytes 131104 | tf_op jit(solution)/shard_map/ppermute | solution.py:248
  11.7 1.7 %copy-done = f32[2,128,2560]{2,1,0:T(8,128)S(1)} copy-done((f32[2,128,2560]{2,1,0:T(8,128)S(1)}, f32[2,128,2560]{2,1,0:T(8,128)}, u32[]{:S(2)}) %copy-start) | copy-done | bytes 2621464
  13.5 1.0 copy-done.1
  14.4 0.9 copy-done.2
  15.4 0.9 copy-done.3
  16.3 13.6 %shard_map.82 = f32[4,2,16,2560]{3,2,1,0:T(8,128)} custom-call(f32[2,128,2560]{2,1,0:T(8,128)S(1)} %copy-done, f32[2,128,128]{2,1,0:T(8,128)S(1)} %collective-permute-done.left_ref, f32[2,128,128]{2,1,0:T(8,128)S(1)} %collective-permute-done.1.right_ref, s32[4,10240]{1,0:T(4,128)S(1)} %copy-done.2, f32[4,10240]{1,0:T(4,128)S(1)} %copy-done.3, ...), custom_call_target="tpu_custom_call" | custom-call | tf_op jit(solution)/shard_map/pallas_call | solution.py:252
  29.9 3.7 %all-to-all-start = ((f32[4,2,16,2560]{3,2,1,0:T(8,128)}), f32[4,2,16,2560]{3,2,1,0:T(8,128)S(1)}, u32[]{:S(2)}, u32[]{:S(2)}) async-start(f32[4,2,16,2560]{3,2,1,0:T(8,128)} %shard_map.82), calls=%async_computation | async-start | bytes 2621440 | tf_op jit(solution)/shard_map/all_to_all | solution.py:267
  33.7 5.2 %constant_dynamic-slice_fusion = f32[2,64,1,1,2560]{4,3,2,1,0:T(1,128)S(1)} fusion(f32[2,64,1,8,2560]{4,3,2,1,0:T(8,128)} %param.12, s32[]{:T(128)S(6)} %select_n.4), kind=kLoop, calls=%fused_computation.5 | loop fusion | bytes 2621444 | tf_op jit(solution)/shard_map/jit(dynamic_index_in_dim)/dynamic_slice | solution.py:268
  38.8 0.0 copy-start.6
  38.8 0.0 copy-start.4
  38.9 0.0 copy-start.5
  38.9 0.1 copy.14
  39.0 0.5 copy-done.6
  39.5 0.1 stack_broadcast_in_dim.2
  39.6 0.0 copy-done.4
  39.6 13.9 %all_gather.3 = s32[3,64,128]{2,1,0:T(8,128)S(1)} all-gather(s32[3,8,128]{2,1,0:T(8,128)S(1)} %pad_add_fusion), channel_id=1, replica_groups=mesh['box'=4,'dir'=8] {'dir'}, dimensions={1}, use_global_device_ids=true | all-gather | bytes 110592 | tf_op jit(solution)/shard_map/all_gather | solution.py:251
  53.5 0.0 all-to-all-done.grid_ref
  53.5 42.8 %shard_map.83 = f32[8,2,8,2560]{3,2,1,0:T(8,128)S(1)} custom-call(f32[4,2,16,2560]{3,2,1,0:T(8,128)S(1)} %all-to-all-done.grid_ref, f32[2,64,2560]{2,1,0:T(8,128)S(1)} %bitcast.14, s32[64,128]{1,0:T(8,128)S(1)} %get-tuple-element.9.ids_ref, s32[64,128]{1,0:T(8,128)S(1)} %get-tuple-element.8.kinds_ref, s32[64,128]{1,0:T(8,128)S(1)} %get-tuple-element.7.lengths_ref), custom_call_target="tpu_custom_call" | custom-call | tf_op jit(solution)/shard_map/pallas_call | solution.py:269
  96.3 34.6 %all_to_all.10 = f32[8,2,8,2560]{3,2,1,0:T(8,128)S(1)} all-to-all(f32[8,2,8,2560]{3,2,1,0:T(8,128)S(1)} %shard_map.83), channel_id=1, replica_groups=mesh['box'=4,'dir'=8] {'dir'}, dimensions={0} | all-to-all | bytes 2621440 | tf_op jit(solution)/shard_map/all_to_all | solution.py:279
  131.0 1.8 %copy.11 = f32[2,8,1,8,2560]{4,3,2,1,0:T(8,128)} copy(f32[2,8,1,8,2560]{4,1,0,3,2:T(8,128)S(1)} %bitcast.15) | data formatting | bytes 2621440 | tf_op jit(solution)/shard_map/broadcast_in_dim | solution.py:280
  (7 shorter events, 0.0 us)
Async XLA Ops:
  1.0 7.1 %collective-permute-start.1 = (f32[2,128,128]{2,1,0:T(8,128)S(1)}, f32[2,128,128]{2,1,0:T(8,128)S(1)}, u32[]{:S(2)}, u32[]{:S(2)}) collective-permute-start(f32[2,128,128]{2,1,0:T(8,128)S(1)} %get-tuple-element.5), channel_id=1, source_target_pairs={{1,0},{2,1},{3,2},{4,3},{5,4},{6,5},{7,6},{0,7},{9,8},{10,9},{11,1... | collective-permute-start | bytes 393224 | tf_op jit(solution)/shard_map/ppermute | solution.py:249
  5.5 6.2 %collective-permute-start = (f32[2,128,128]{2,1,0:T(8,128)S(1)}, f32[2,128,128]{2,1,0:T(8,128)S(1)}, u32[]{:S(2)}, u32[]{:S(2)}) collective-permute-start(f32[2,128,128]{2,1,0:T(8,128)S(1)} %get-tuple-element.6), channel_id=1, source_target_pairs={{0,1},{1,2},{2,3},{3,4},{4,5},{5,6},{6,7},{7,0},{8,9},{9,10},{10,1... | collective-permute-start | bytes 393224 | tf_op jit(solution)/shard_map/ppermute | solution.py:248
  11.7 1.7 %copy-start = (f32[2,128,2560]{2,1,0:T(8,128)S(1)}, f32[2,128,2560]{2,1,0:T(8,128)}, u32[]{:S(2)}) copy-start(f32[2,128,2560]{2,1,0:T(8,128)} %children_ref.1) | copy-start | bytes 7864324
  13.5 1.0 copy-start.1
  14.4 0.9 copy-start.2
  15.4 0.9 copy-start.3
  29.9 23.6 %all-to-all-start = ((f32[4,2,16,2560]{3,2,1,0:T(8,128)}), f32[4,2,16,2560]{3,2,1,0:T(8,128)S(1)}, u32[]{:S(2)}, u32[]{:S(2)}) async-start(f32[4,2,16,2560]{3,2,1,0:T(8,128)} %shard_map.82), calls=%async_computation | async-start | bytes 2621440 | tf_op jit(solution)/shard_map/all_to_all | solution.py:267
  38.8 0.7 copy-start.6
  38.8 0.7 copy-start.4
  38.9 0.7 copy-start.5

commit v2 on v1

v2 whole, which is shorter than its diff:
```python
import functools

import jax
import jax.numpy as jnp
from jax import lax
from jax.experimental import pallas as pl
from jax.experimental.pallas import tpu as pltpu
from jax.sharding import PartitionSpec as P

LANES = 128
F32 = jnp.float32
BF16 = jnp.bfloat16
SIN_TERMS = (1.0, -1 / 6, 1 / 120, -1 / 5040, 1 / 362880, -1 / 39916800, 1 / 6227020800)
COS_TERMS = (1.0, -1 / 2, 1 / 24, -1 / 720, 1 / 40320, -1 / 3628800, 1 / 479001600)


def split(value):
    high = value.astype(BF16)
    return high, (value - high.astype(F32)).astype(BF16)


def series(terms, square):
    total = jnp.full_like(square, terms[-1])
    for term in terms[-2::-1]:
        total = total * square + term
    return total


def sine_cosine(angle):
    half = angle * 0.5
    square = half * half
    sine = half * series(SIN_TERMS, square)
    cosine = series(COS_TERMS, square)
    return 2.0 * sine * cosine, 1.0 - 2.0 * sine * sine


def shifted_tile(before, tile):
    lane = lax.broadcasted_iota(jnp.int32, tile.shape, 1)
    return jnp.where(lane < 2, pltpu.roll(before, 2, axis=1), pltpu.roll(tile, 2, axis=1))


def rows_of(ref, part, octant, parents):
    return ref[part, pl.ds(octant, parents, stride=8), :]


def prepare_columns(held_ref, left_ref, right_ref, tile, high_ref, low_ref, parents):
    tiles = held_ref.shape[0]
    edge = isinstance(tile, int)
    here = right_ref if edge and tile == tiles else held_ref.at[tile]
    before = left_ref if edge and tile == 0 else held_ref.at[tile - 1]
    column = tile * LANES if edge else pl.multiple_of(tile * LANES, LANES)
    for octant in range(8):
        for part in range(2):
            moved = shifted_tile(
                rows_of(before, part, octant, parents), rows_of(here, part, octant, parents)
            )
            high, low = split(moved)
            rows = pl.ds((octant * 2 + part) * parents, parents)
            high_ref[rows, pl.ds(column, LANES)] = high
            low_ref[rows, pl.ds(column, LANES)] = low


def block_layout(width, span):
    block = 512 if span % 512 == 0 else span
    return block, (256 if block == 512 else -(-(block // 4 + 128) // LANES) * LANES)


def band_matrix(index_ref, weight_ref, start, first, shift, block, total, high_ref, low_ref):
    lane = lax.broadcasted_iota(jnp.int32, (1, LANES), 1) // 4
    row = lax.broadcasted_iota(jnp.int32, (48, LANES), 0)
    for tile in range(block // LANES):
        column = pl.multiple_of(start + tile * LANES, LANES)
        centre = (first + start + tile * LANES) // 4 + lane
        band = jnp.zeros((48, LANES), F32)
        for point in range(index_ref.shape[0]):
            offset = index_ref[pl.ds(point, 1), pl.ds(column, LANES)] - centre + 2
            offset = jnp.where(offset < 0, offset + total, offset)
            offset = jnp.where(offset >= total, offset - total, offset) + lane
            band = band + jnp.where(row == offset, weight_ref[pl.ds(point, 1), pl.ds(column, LANES)], 0.0)
        high, low = split(band)
        rows = pl.ds(pl.multiple_of(shift + tile * 32, 32), 48)
        high_ref[rows, pl.ds(tile * LANES, LANES)] = high
        low_ref[rows, pl.ds(tile * LANES, LANES)] = low


def aggregate_block(refs, start, base, shift, first, block, total, parents, out_ref):
    index_ref, weight_ref, phase_ref, high_ref, low_ref, band_high, band_low, fine_ref = refs
    depth = band_high.shape[0]
    band_matrix(index_ref, weight_ref, start, first, shift, block, total, band_high, band_low)
    window = pl.ds(base, depth)
    lhs = jnp.concatenate([high_ref[:, window], high_ref[:, window], low_ref[:, window]], axis=1)
    rhs = jnp.concatenate([band_high[...], band_low[...], band_high[...]], axis=0)
    fine_ref[...] = jnp.dot(lhs, rhs, preferred_element_type=F32)
    for tile in range(block // LANES):
        lanes = pl.ds(tile * LANES, LANES)
        sine, cosine = sine_cosine(phase_ref[:, pl.ds(pl.multiple_of(start + tile * LANES, LANES), LANES)])
        real = jnp.zeros((parents, LANES), F32)
        imag = jnp.zeros((parents, LANES), F32)
        for octant in range(8):
            s, c = sine[octant : octant + 1], cosine[octant : octant + 1]
            fine_real = fine_ref[pl.ds(octant * 2 * parents, parents), lanes]
            fine_imag = fine_ref[pl.ds((octant * 2 + 1) * parents, parents), lanes]
            real = real + (fine_real * c - fine_imag * s)
            imag = imag + (fine_real * s + fine_imag * c)
        out_ref[0, :, lanes] = real
        out_ref[1, :, lanes] = imag


def count_pairs(lists_ref, kinds, sources, loose_ref, counts_ref):
    slots = lists_ref.shape[3]
    slot = lax.broadcasted_iota(jnp.int32, (1, slots), 1)
    kind = lax.broadcasted_iota(jnp.int32, (kinds, slots), 0)
    source = lax.broadcasted_iota(jnp.int32, (2 * sources, slots), 0) % sources

    @pl.loop(0, counts_ref.shape[0])
    def _(d):
        for p in range(8):
            live = slot < lists_ref[d, 2, pl.ds(p, 1), :]
            kind_hot = ((kind == lists_ref[d, 1, pl.ds(p, 1), :]) & live).astype(F32).astype(BF16)
            source_hot = (source == lists_ref[d, 0, pl.ds(p, 1), :]).astype(F32).astype(BF16)
            pairs = lax.dot_general(
                kind_hot, source_hot, (((1,), (1,)), ((), ())), preferred_element_type=F32
            )
            for part in range(loose_ref.shape[0]):
                loose_ref[part, pl.ds(p, kinds, stride=8), :] = pairs[:, part * LANES : (part + 1) * LANES]
        for part in range(loose_ref.shape[0]):
            counts_ref[d, :, pl.ds(part * LANES, LANES)] = loose_ref[part].astype(BF16)


def load_sources(grid_ref, sources_ref):
    blocks, _, parents, _ = grid_ref.shape
    sources = blocks * parents
    for tile in range(sources_ref.shape[0]):
        lanes = pl.ds(tile * LANES, LANES)
        for b in range(blocks):
            for part in range(2):
                high, low = split(grid_ref[b, part, :, lanes])
                columns = pl.ds(part * LANES, LANES)
                sources_ref[tile, pl.ds(b * parents, parents), columns] = high
                sources_ref[tile, pl.ds(sources + b * parents, parents), columns] = low


def spread_table(table_ref, column, wide_ref):
    @pl.loop(0, table_ref.shape[1] // 8)
    def _(group):
        for tile in range(wide_ref.shape[0]):
            lanes = pl.ds(pl.multiple_of(column + tile * LANES, LANES), LANES)
            for part in range(2):
                for k in range(8):
                    row = table_ref[part, pl.ds(pl.multiple_of(group * 8, 8), 8), lanes][k : k + 1]
                    wide_ref[tile, part, group * 8 + k] = jnp.broadcast_to(row, (8, LANES))


def multiply_tile(summed_ref, wide_ref, tile, out_ref):
    real = jnp.zeros((8, LANES), F32)
    imag = jnp.zeros((8, LANES), F32)
    for k in range(wide_ref.shape[2]):
        table_real, table_imag = wide_ref[tile, 0, k], wide_ref[tile, 1, k]
        summed_real = summed_ref[pl.ds(k * 8, 8), pl.ds(0, LANES)]
        summed_imag = summed_ref[pl.ds(k * 8, 8), pl.ds(LANES, LANES)]
        real = real + (table_real * summed_real - table_imag * summed_imag)
        imag = imag + (table_real * summed_imag + table_imag * summed_real)
    out_ref[0, :, pl.ds(tile * LANES, LANES)] = real
    out_ref[1, :, pl.ds(tile * LANES, LANES)] = imag


def fused_kernel(
    parents, span, total, lists_in, children_ref, index_in, weight_in, phase_in, table_in, out_ref,
    held_ref, left_ref, right_ref, index_ref, weight_ref, phase_ref, table_ref, lists_ref,
    high_ref, low_ref, band_high, band_low, fine_ref, outgoing_ref, grid_ref,
    loose_ref, counts_ref, sources_ref, wide_ref, summed_even, summed_odd, result_ref,
    load_sems, input_sems, self_sems, halo_send, halo_recv, list_send, list_recv,
    box_send, box_recv, dir_send, dir_recv,
):
    tiles = held_ref.shape[0]
    chunks, boxes, _, _, block = grid_ref.shape
    dirs = lists_ref.shape[0]
    kinds = table_ref.shape[1]
    depth = band_high.shape[0]
    my_box, my_dir = lax.axis_index("box"), lax.axis_index("dir")
    first = my_dir * index_ref.shape[1]
    mesh_type = pl.DeviceIdType.MESH

    def dir_at(step):
        return (my_dir + step + dirs) % dirs

    def box_at(step):
        return (my_box + step + boxes) % boxes

    inputs = [
        pltpu.make_async_copy(source, target, input_sems.at[i])
        for i, (source, target) in enumerate(
            [
                (index_in, index_ref), (weight_in, weight_ref), (phase_in, phase_ref),
                (lists_in, lists_ref.at[my_dir]), (table_in.at[:, :, 0, my_dir], table_ref),
            ]
        )
    ]

    def load(tile):
        return pltpu.make_async_copy(
            children_ref.at[:, :, pl.ds(pl.multiple_of(tile * LANES, LANES), LANES)],
            held_ref.at[tile], load_sems.at[tile],
        )

    @pl.loop(0, tiles)
    def _(tile):
        load(tile).start()

    for copy in inputs:
        copy.start()

    barrier = pltpu.get_barrier_semaphore()

    @pl.loop(1, dirs)
    def _(step):
        pl.semaphore_signal(barrier, inc=1, device_id={"dir": dir_at(step)}, device_id_type=mesh_type)

    @pl.loop(1, boxes)
    def _(step):
        pl.semaphore_signal(barrier, inc=1, device_id={"box": box_at(step)}, device_id_type=mesh_type)

    pl.semaphore_wait(barrier, dirs + boxes - 2)

    halos = [
        pltpu.make_async_remote_copy(
            src_ref=children_ref.at[:, :, pl.ds(column, LANES)], dst_ref=target,
            send_sem=halo_send.at[i], recv_sem=halo_recv.at[i],
            device_id={"dir": dir_at(step)}, device_id_type=mesh_type,
        )
        for i, (column, target, step) in enumerate(
            [((tiles - 1) * LANES, left_ref, 1), (0, right_ref, -1)]
        )
    ]
    for copy in halos:
        copy.start()

    def list_copy(step, owner):
        return pltpu.make_async_remote_copy(
            src_ref=lists_in, dst_ref=lists_ref.at[owner],
            send_sem=list_send.at[step], recv_sem=list_recv.at[step],
            device_id={"dir": dir_at(step)}, device_id_type=mesh_type,
        )

    @pl.loop(1, dirs)
    def _(step):
        list_copy(step, my_dir).start()

    def box_copy(chunk, step, owner):
        return pltpu.make_async_remote_copy(
            src_ref=outgoing_ref.at[chunk, step], dst_ref=grid_ref.at[chunk, owner],
            send_sem=box_send.at[chunk, step], recv_sem=box_recv.at[chunk, step],
            device_id={"box": box_at(step)}, device_id_type=mesh_type,
        )

    def own_box_copy(chunk):
        return pltpu.make_async_copy(
            outgoing_ref.at[chunk, 0], grid_ref.at[chunk, my_box], self_sems.at[0, chunk]
        )

    def dir_target(chunk, owner):
        return out_ref.at[owner, :, :, pl.ds(pl.multiple_of(chunk * block, LANES), block)]

    def dir_copy(chunk, step, owner):
        return pltpu.make_async_remote_copy(
            src_ref=result_ref.at[chunk, step], dst_ref=dir_target(chunk, owner),
            send_sem=dir_send.at[chunk, step], recv_sem=dir_recv.at[chunk, step],
            device_id={"dir": dir_at(step)}, device_id_type=mesh_type,
        )

    def own_dir_copy(chunk):
        return pltpu.make_async_copy(
            result_ref.at[chunk, 0], dir_target(chunk, my_dir), self_sems.at[1, chunk]
        )

    def clear():
        band_high[...] = jnp.zeros_like(band_high)
        band_low[...] = jnp.zeros_like(band_low)

    clear()

    @pl.loop(0, tiles)
    def _(tile):
        load(tile).wait()

    @pl.loop(1, tiles)
    def _(tile):
        prepare_columns(held_ref, left_ref, right_ref, tile, high_ref, low_ref, parents)

    def edges():
        for copy in halos:
            copy.wait_recv()
        prepare_columns(held_ref, left_ref, right_ref, 0, high_ref, low_ref, parents)
        prepare_columns(held_ref, left_ref, right_ref, tiles, high_ref, low_ref, parents)

    def lists():
        inputs[3].wait()

        @pl.loop(1, dirs)
        def _(step):
            list_copy(step, dir_at(-step)).wait_recv()

        count_pairs(lists_ref, kinds, sources_ref.shape[1] // 2, loose_ref, counts_ref)
        inputs[4].wait()

    for copy in inputs[:3]:
        copy.wait()

    refs = (index_ref, weight_ref, phase_ref, high_ref, low_ref, band_high, band_low, fine_ref)

    def aggregate(chunk):
        @pl.loop(0, boxes)
        def _(turn):
            step = (turn + 1) % boxes
            start = pl.multiple_of(box_at(step) * span + chunk * block, LANES)
            coarse = start // 4
            if block == 512:
                base, shift = pl.multiple_of(coarse, LANES), 0
            else:
                clear()
                base = pl.multiple_of(coarse // LANES * LANES, LANES)
                shift = coarse % LANES
            aggregate_block(
                refs, start, base, shift, first, block, total, parents, outgoing_ref.at[chunk, step]
            )

            @pl.when(step > 0)
            def _():
                box_copy(chunk, step, my_box).start()

        own_box_copy(chunk).start()

    def translate(chunk):
        spread_table(table_ref, chunk * block, wide_ref)
        own_box_copy(chunk).wait()

        @pl.loop(1, boxes)
        def _(step):
            box_copy(chunk, step, box_at(-step)).wait_recv()

        load_sources(grid_ref.at[chunk], sources_ref)
        count = sources_ref.shape[0]
        buffers = (summed_even, summed_odd)

        def sum_tile(d, tile, buffer):
            buffer[...] = jnp.dot(counts_ref[d], sources_ref[tile], preferred_element_type=F32)

        def items(step, parity):
            for tile in range(count):
                if tile + 1 < count:
                    sum_tile(dir_at(step), tile + 1, buffers[(parity + tile + 1) % 2])
                else:
                    sum_tile(dir_at(step + 1), 0, buffers[(parity + tile + 1) % 2])
                multiply_tile(buffers[(parity + tile) % 2], wide_ref, tile, result_ref.at[chunk, step])

        def send(step):
            @pl.when(step > 0)
            def _():
                dir_copy(chunk, step, my_dir).start()

        sum_tile(dir_at(1), 0, summed_even)
        if count % 2 == 0:

            @pl.loop(0, dirs)
            def _(turn):
                step = (turn + 1) % dirs
                items(step, 0)
                send(step)

        else:

            @pl.loop(0, dirs // 2)
            def _(turn):
                for half in range(2):
                    step = (2 * turn + half + 1) % dirs
                    items(step, half)
                    send(step)

        own_dir_copy(chunk).start()

    if chunks < 3:
        edges()

    @pl.loop(0, chunks + 1)
    def _(turn):
        @pl.when(turn < chunks)
        def _():
            aggregate((turn + 1) % chunks)

        @pl.when(turn == 0)
        def _():
            if chunks >= 3:
                edges()
            lists()

        @pl.when(turn > 0)
        def _():
            translate(turn % chunks)

    for copy in halos:
        copy.wait_send()

    @pl.loop(1, dirs)
    def _(step):
        list_copy(step, my_dir).wait_send()

    @pl.loop(0, chunks)
    def _(chunk):
        own_dir_copy(chunk).wait()

        @pl.loop(1, boxes)
        def _(step):
            box_copy(chunk, step, my_box).wait_send()

        @pl.loop(1, dirs)
        def _(step):
            dir_copy(chunk, step, my_dir).wait_send()
            dir_copy(chunk, step, dir_at(-step)).wait_recv()


def on_device(
    children, stencil_index, stencil_weights, child_phase, translations, box_lengths, partner_ids, partner_kinds
):
    boxes = lax.axis_size("box")
    dirs = lax.axis_size("dir")
    rows, coarse = children.shape[1:]
    fine = stencil_index.shape[1]
    parents = rows // 8
    span = fine // boxes
    kinds = translations.shape[1]
    sources = parents * boxes
    slots = partner_ids.shape[1]
    block, depth = block_layout(fine, span)
    chunks = span // block
    lengths = jnp.broadcast_to(box_lengths[:, None], partner_ids.shape)
    lists = jnp.stack([partner_ids, partner_kinds, lengths])
    vmem, dma = pltpu.VMEM, pltpu.SemaphoreType.DMA
    result = pl.pallas_call(
        functools.partial(fused_kernel, parents, span, coarse * dirs),
        out_shape=jax.ShapeDtypeStruct((dirs, 2, 8, span), F32),
        in_specs=[pl.BlockSpec(memory_space=pl.ANY)] * 6,
        out_specs=pl.BlockSpec(memory_space=pl.ANY),
        scratch_shapes=[
            vmem((coarse // LANES, 2, rows, LANES), F32),
            vmem((2, rows, LANES), F32),
            vmem((2, rows, LANES), F32),
            vmem(stencil_index.shape, jnp.int32),
            vmem(stencil_weights.shape, F32),
            vmem(child_phase.shape, F32),
            vmem((2, kinds, span), F32),
            vmem((dirs, 3, 8, slots), jnp.int32),
            vmem((2 * rows, coarse + LANES), BF16),
            vmem((2 * rows, coarse + LANES), BF16),
            vmem((depth, block), BF16),
            vmem((depth, block), BF16),
            vmem((2 * rows, block), F32),
            vmem((chunks, boxes, 2, parents, block), F32),
            vmem((chunks, boxes, 2, parents, block), F32),
            vmem((2 * sources // LANES, kinds * 8, LANES), F32),
            vmem((dirs, kinds * 8, 2 * sources), BF16),
            vmem((block // LANES, 2 * sources, 2 * LANES), BF16),
            vmem((block // LANES, 2, kinds, 8, LANES), F32),
            vmem((kinds * 8, 2 * LANES), F32),
            vmem((kinds * 8, 2 * LANES), F32),
            vmem((chunks, dirs, 2, 8, block), F32),
            dma((coarse // LANES,)),
            dma((5,)),
            dma((2, chunks)),
            dma((2,)),
            dma((2,)),
            dma((dirs,)),
            dma((dirs,)),
            dma((chunks, boxes)),
            dma((chunks, boxes)),
            dma((chunks, dirs)),
            dma((chunks, dirs)),
        ],
        compiler_params=pltpu.CompilerParams(
            collective_id=0, has_side_effects=True, vmem_limit_bytes=56 << 20
        ),
    )(lists, children, stencil_index, stencil_weights, child_phase, translations)
    return jnp.transpose(result, (1, 2, 0, 3))[:, :, None]


def solution(mesh):
    return jax.shard_map(
        on_device,
        mesh=mesh,
        in_specs=(
            P(None, "box", "dir"),
            P(None, "dir"),
            P(None, "dir"),
            P(None, "dir"),
            P(None, None, "box", None, None),
            P("dir"),
            P("dir", None),
            P("dir", None),
        ),
        out_specs=P(None, "dir", "box", None, None),
        check_vma=False,
    )
```

time: 133 us -> 55.4 us (0.42)
  blocking collectives: 48.6 us -> 0 us
  local copies, waits for them, and re-layouts: 13.2 us -> 3.86 us
  starting transfers between devices: 8.28 us -> 0 us
  Pallas kernels: 56.4 us -> 49.9 us
  waiting for transfers between devices: 6.19 us -> 0 us
    all_to_all x1 -> x0, blocking collectives: 34.6 us -> none  [on_device(): lax.all_to_all(result, 'dir', split_axis=0, concat_axis=0, tiled=True)]
    all_gather x1 -> x0, blocking collectives: 13.9 us -> none  [on_device(): lax.all_gather(jnp.stack([partner_ids, partner_kinds, lengths]), 'dir', a...]
    pallas_call x2 -> x1, Pallas kernels: 56.4 us -> 49.9 us  [on_device(): pl.pallas_call(functools.partial(fused_kernel, parents, span, coarse * di...]
    ppermute x2 -> x0, waiting for transfers between devices: 6.19 us -> none  [the longest x1 3.67 us: on_device(): left = lax.ppermute(children[:, :, coarse - LANES:], 'dir', forward)]
    unnamed x15 -> x0, local copies, waits for them, and re-layouts: 5.17 us -> none
    dynamic_slice x1 -> x0, local copies, waits for them, and re-layouts: 5.17 us -> none  [on_device(): lax.dynamic_index_in_dim(translations[:, :, 0], lax.axis_index('dir'), ax...]
    ppermute x2 -> x0, starting transfers between devices: 4.54 us -> none  [the longest x1 4.54 us: on_device(): right = lax.ppermute(children[:, :, :LANES], 'dir', backward)]
    all_to_all x1 -> x0, starting transfers between devices: 3.73 us -> none  [on_device(): lax.all_to_all(outgoing, 'box', split_axis=0, concat_axis=0, tiled=True)]
  transfers between devices with their start and end apart: 3 -> 0, of which waited for: 2 -> 0; matrix products, arithmetic and copies ran while one was open for 4% -> 0% of each run, Pallas kernels for 0% -> 0%
where the time goes in v2:
time: 55.4 us; the launch traced here: 55.1 us
  Pallas kernels  49.9 us (90%)
  local copies, waits for them, and re-layouts  3.86 us (7%)
  other arithmetic  1.3 us (2%)
    pallas_call x1, Pallas kernels, on_device(): pl.pallas_call(functools.partial(fused_kernel, parents, span, coarse * di...  49.9 us
    broadcast_in_dim x1, local copies, waits for them, and re-layouts, on_device(): return jnp.transpose(result, (1, 2, 0, 3))[:, :, None]  3.14 us
    another operation x1, other arithmetic, on_device(): lists = jnp.stack([partner_ids, partner_kinds, lengths])  1.3 us

profile of v2, /device:TPU:0, one launch (start us, length us, event | category | flops | bytes accessed | tf_op | source)
XLA Modules:
  0.0 55.1 jit_solution(3615733764746577675)
XLA Ops:
  0.0 0.7 %stack_broadcast_in_dim.2 = s32[1,8,128]{2,1,0:T(8,128)S(1)} broadcast(s32[8]{0:T(128)} %param.13), dimensions={1} | broadcast | bytes 4128 | tf_op jit(solution)/shard_map/stack;broadcast_in_dim | solution.py:436
  0.7 1.3 %pad_add_fusion.lists_in = s32[3,8,128]{2,1,0:T(8,128)} fusion(s32[1,8,128]{2,1,0:T(8,128)S(1)} %stack_broadcast_in_dim.2, s32[1,8,128]{2,1,0:T(8,128)} %bitcast.6, s32[1,8,128]{2,1,0:T(8,128)} %bitcast.7), kind=kLoop, calls=%fused_computation | loop fusion | flops 6144 | bytes 24576 | tf_op jit(solution)/shard_map/stack | solution.py:436
  2.0 49.9 %shard_map.82 = f32[8,2,8,2560]{3,2,1,0:T(8,128)} custom-call(s32[3,8,128]{2,1,0:T(8,128)} %pad_add_fusion.lists_in, f32[2,128,2560]{2,1,0:T(8,128)} %children_ref.1, s32[4,10240]{1,0:T(4,128)} %index_in.1, f32[4,10240]{1,0:T(4,128)} %weight_in.1, f32[8,10240]{1,0:T(8,128)} %phase_in.1, f32[2,64,1,8,2560]{4,3,2,1,0:T(8,128)} %table_in.1), custom_call_target="tpu_custom_call" | custom-call | tf_op jit(solution)/shard_map/pallas_call | solution.py:438
  52.0 3.1 %copy.9 = f32[2,8,1,8,2560]{4,3,2,1,0:T(8,128)} copy(f32[2,8,1,8,2560]{4,1,0,3,2:T(8,128)} %bitcast.5) | data formatting | bytes 2621440 | tf_op jit(solution)/shard_map/broadcast_in_dim | solution.py:482

commit v3 on v2

--- a/solution.py
+++ b/solution.py
@@ -83,15 +83,15 @@
         low_ref[rows, pl.ds(tile * LANES, LANES)] = low
 
 
-def aggregate_block(refs, start, base, shift, first, block, total, parents, out_ref):
-    index_ref, weight_ref, phase_ref, high_ref, low_ref, band_high, band_low, fine_ref = refs
-    depth = band_high.shape[0]
-    band_matrix(index_ref, weight_ref, start, first, shift, block, total, band_high, band_low)
-    window = pl.ds(base, depth)
+def interpolate(high_ref, low_ref, base, band_high, band_low, fine_ref):
+    window = pl.ds(base, band_high.shape[0])
     lhs = jnp.concatenate([high_ref[:, window], high_ref[:, window], low_ref[:, window]], axis=1)
     rhs = jnp.concatenate([band_high[...], band_low[...], band_high[...]], axis=0)
     fine_ref[...] = jnp.dot(lhs, rhs, preferred_element_type=F32)
-    for tile in range(block // LANES):
+
+
+def rotate(phase_ref, start, fine_ref, parents, out_ref):
+    for tile in range(fine_ref.shape[1] // LANES):
         lanes = pl.ds(tile * LANES, LANES)
         sine, cosine = sine_cosine(phase_ref[:, pl.ds(pl.multiple_of(start + tile * LANES, LANES), LANES)])
         real = jnp.zeros((parents, LANES), F32)
@@ -165,18 +165,17 @@
 
 
 def fused_kernel(
-    parents, span, total, lists_in, children_ref, index_in, weight_in, phase_in, table_in, out_ref,
-    held_ref, left_ref, right_ref, index_ref, weight_ref, phase_ref, table_ref, lists_ref,
-    high_ref, low_ref, band_high, band_low, fine_ref, outgoing_ref, grid_ref,
-    loose_ref, counts_ref, sources_ref, wide_ref, summed_even, summed_odd, result_ref,
+    parents, span, total, ids_in, kinds_in, lengths_in, children_ref, index_in, weight_in, phase_in, table_in, out_ref,
+    held_ref, left_ref, right_ref, index_ref, weight_ref, phase_ref, table_ref, lists_ref, spare_ref,
+    high_ref, low_ref, high_a, low_a, fine_a, high_b, low_b, fine_b, outgoing_ref, grid_ref,
+    loose_ref, counts_ref, sources_ref, wide_ref, summed_even, summed_odd, result_ref, landing_ref,
     load_sems, input_sems, self_sems, halo_send, halo_recv, list_send, list_recv,
-    box_send, box_recv, dir_send, dir_recv,
+    box_send, box_recv, dir_send, dir_recv, place_sems,
 ):
     tiles = held_ref.shape[0]
     chunks, boxes, _, _, block = grid_ref.shape
     dirs = lists_ref.shape[0]
     kinds = table_ref.shape[1]
-    depth = band_high.shape[0]
     my_box, my_dir = lax.axis_index("box"), lax.axis_index("dir")
     first = my_dir * index_ref.shape[1]
     mesh_type = pl.DeviceIdType.MESH
@@ -192,7 +191,8 @@
         for i, (source, target) in enumerate(
             [
                 (index_in, index_ref), (weight_in, weight_ref), (phase_in, phase_ref),
-                (lists_in, lists_ref.at[my_dir]), (table_in.at[:, :, 0, my_dir], table_ref),
+                (ids_in, lists_ref.at[my_dir, 0]), (kinds_in, lists_ref.at[my_dir, 1]),
+                (lengths_in, spare_ref), (table_in.at[:, :, 0, my_dir], table_ref),
             ]
         )
     ]
@@ -237,10 +237,17 @@
 
     def list_copy(step, owner):
         return pltpu.make_async_remote_copy(
-            src_ref=lists_in, dst_ref=lists_ref.at[owner],
+            src_ref=lists_ref.at[my_dir], dst_ref=lists_ref.at[owner],
             send_sem=list_send.at[step], recv_sem=list_recv.at[step],
             device_id={"dir": dir_at(step)}, device_id_type=mesh_type,
         )
+
+    for copy in inputs[3:6]:
+        copy.wait()
+    square = (8, spare_ref.shape[1])
+    own = lax.broadcasted_iota(jnp.int32, square, 0) == lax.broadcasted_iota(jnp.int32, square, 1)
+    lengths = jnp.sum(jnp.where(own, spare_ref[...].astype(F32), 0.0), axis=1, keepdims=True)
+    lists_ref[my_dir, 2] = jnp.broadcast_to(lengths, (8, lists_ref.shape[3])).astype(jnp.int32)
 
     @pl.loop(1, dirs)
     def _(step):
@@ -259,7 +266,14 @@
         )
 
     def dir_target(chunk, owner):
-        return out_ref.at[owner, :, :, pl.ds(pl.multiple_of(chunk * block, LANES), block)]
+        return landing_ref.at[owner, :, :, pl.ds(pl.multiple_of(chunk * block, LANES), block)]
+
+    def place(chunk, step):
+        lanes = pl.ds(pl.multiple_of(chunk * block, LANES), block)
+        return pltpu.make_async_copy(
+            dir_target(chunk, dir_at(-step)), out_ref.at[:, :, 0, dir_at(-step), lanes],
+            place_sems.at[chunk, step],
+        )
 
     def dir_copy(chunk, step, owner):
         return pltpu.make_async_remote_copy(
@@ -274,8 +288,8 @@
         )
 
     def clear():
-        band_high[...] = jnp.zeros_like(band_high)
-        band_low[...] = jnp.zeros_like(band_low)
+        for ref in (high_a, low_a, high_b, low_b):
+            ref[...] = jnp.zeros_like(ref)
 
     clear()
 
@@ -294,39 +308,43 @@
         prepare_columns(held_ref, left_ref, right_ref, tiles, high_ref, low_ref, parents)
 
     def lists():
-        inputs[3].wait()
-
         @pl.loop(1, dirs)
         def _(step):
             list_copy(step, dir_at(-step)).wait_recv()
 
         count_pairs(lists_ref, kinds, sources_ref.shape[1] // 2, loose_ref, counts_ref)
-        inputs[4].wait()
+        inputs[6].wait()
 
     for copy in inputs[:3]:
         copy.wait()
 
-    refs = (index_ref, weight_ref, phase_ref, high_ref, low_ref, band_high, band_low, fine_ref)
-
     def aggregate(chunk):
-        @pl.loop(0, boxes)
-        def _(turn):
-            step = (turn + 1) % boxes
-            start = pl.multiple_of(box_at(step) * span + chunk * block, LANES)
-            coarse = start // 4
-            if block == 512:
-                base, shift = pl.multiple_of(coarse, LANES), 0
-            else:
+        @pl.loop(0, boxes // 2)
+        def _(pair):
+            steps = (2 * pair + 1, (2 * pair + 2) % boxes)
+            if block != 512:
                 clear()
-                base = pl.multiple_of(coarse // LANES * LANES, LANES)
-                shift = coarse % LANES
-            aggregate_block(
-                refs, start, base, shift, first, block, total, parents, outgoing_ref.at[chunk, step]
-            )
-
-            @pl.when(step > 0)
+            work = []
+            for step, buffers in zip(steps, ((high_a, low_a, fine_a), (high_b, low_b, fine_b))):
+                start = pl.multiple_of(box_at(step) * span + chunk * block, LANES)
+                coarse = start // 4
+                if block == 512:
+                    base, shift = pl.multiple_of(coarse, LANES), 0
+                else:
+                    base = pl.multiple_of(coarse // LANES * LANES, LANES)
+                    shift = coarse % LANES
+                work.append((start, base, shift, step) + buffers)
+            for start, base, shift, step, band_high, band_low, fine_ref in work:
+                band_matrix(index_ref, weight_ref, start, first, shift, block, total, band_high, band_low)
+            for start, base, shift, step, band_high, band_low, fine_ref in work:
+                interpolate(high_ref, low_ref, base, band_high, band_low, fine_ref)
+            for start, base, shift, step, band_high, band_low, fine_ref in work:
+                rotate(phase_ref, start, fine_ref, parents, outgoing_ref.at[chunk, step])
+            box_copy(chunk, steps[0], my_box).start()
+
+            @pl.when(steps[1] > 0)
             def _():
-                box_copy(chunk, step, my_box).start()
+                box_copy(chunk, steps[1], my_box).start()
 
         own_box_copy(chunk).start()
 
@@ -383,14 +401,15 @@
 
     @pl.loop(0, chunks + 1)
     def _(turn):
+        if chunks >= 3:
+            pl.when(turn == chunks - 2)(edges)
+
         @pl.when(turn < chunks)
         def _():
             aggregate((turn + 1) % chunks)
 
         @pl.when(turn == 0)
         def _():
-            if chunks >= 3:
-                edges()
             lists()
 
         @pl.when(turn > 0)
@@ -405,17 +424,29 @@
         list_copy(step, my_dir).wait_send()
 
     @pl.loop(0, chunks)
-    def _(chunk):
+    def _(turn):
+        chunk = (turn + 1) % chunks
         own_dir_copy(chunk).wait()
+        place(chunk, 0).start()
+
+        @pl.loop(1, dirs)
+        def _(step):
+            dir_copy(chunk, step, dir_at(-step)).wait_recv()
+            place(chunk, step).start()
 
         @pl.loop(1, boxes)
         def _(step):
             box_copy(chunk, step, my_box).wait_send()
 
+    @pl.loop(0, chunks)
+    def _(chunk):
         @pl.loop(1, dirs)
         def _(step):
             dir_copy(chunk, step, my_dir).wait_send()
-            dir_copy(chunk, step, dir_at(-step)).wait_recv()
+
+        @pl.loop(0, dirs)
+        def _(step):
+            place(chunk, step).wait()
 
 
 def on_device(
@@ -432,13 +463,11 @@
     slots = partner_ids.shape[1]
     block, depth = block_layout(fine, span)
     chunks = span // block
-    lengths = jnp.broadcast_to(box_lengths[:, None], partner_ids.shape)
-    lists = jnp.stack([partner_ids, partner_kinds, lengths])
     vmem, dma = pltpu.VMEM, pltpu.SemaphoreType.DMA
-    result = pl.pallas_call(
+    return pl.pallas_call(
         functools.partial(fused_kernel, parents, span, coarse * dirs),
-        out_shape=jax.ShapeDtypeStruct((dirs, 2, 8, span), F32),
-        in_specs=[pl.BlockSpec(memory_space=pl.ANY)] * 6,
+        out_shape=jax.ShapeDtypeStruct((2, 8, 1, dirs, span), F32),
+        in_specs=[pl.BlockSpec(memory_space=pl.ANY)] * 8,
         out_specs=pl.BlockSpec(memory_space=pl.ANY),
         scratch_shapes=[
             vmem((coarse // LANES, 2, rows, LANES), F32),
@@ -449,8 +478,12 @@
             vmem(child_phase.shape, F32),
             vmem((2, kinds, span), F32),
             vmem((dirs, 3, 8, slots), jnp.int32),
+            vmem((1, box_lengths.shape[0]), jnp.int32),
             vmem((2 * rows, coarse + LANES), BF16),
             vmem((2 * rows, coarse + LANES), BF16),
+            vmem((depth, block), BF16),
+            vmem((depth, block), BF16),
+            vmem((2 * rows, block), F32),
             vmem((depth, block), BF16),
             vmem((depth, block), BF16),
             vmem((2 * rows, block), F32),
@@ -463,8 +496,9 @@
             vmem((kinds * 8, 2 * LANES), F32),
             vmem((kinds * 8, 2 * LANES), F32),
             vmem((chunks, dirs, 2, 8, block), F32),
+            vmem((dirs, 2, 8, span), F32),
             dma((coarse // LANES,)),
-            dma((5,)),
+            dma((7,)),
             dma((2, chunks)),
             dma((2,)),
             dma((2,)),
@@ -474,12 +508,12 @@
             dma((chunks, boxes)),
             dma((chunks, dirs)),
             dma((chunks, dirs)),
+            dma((chunks, dirs)),
         ],
         compiler_params=pltpu.CompilerParams(
             collective_id=0, has_side_effects=True, vmem_limit_bytes=56 << 20
         ),
-    )(lists, children, stencil_index, stencil_weights, child_phase, translations)
-    return jnp.transpose(result, (1, 2, 0, 3))[:, :, None]
+    )(partner_ids, partner_kinds, box_lengths.reshape(1, -1), children, stencil_index, stencil_weights, child_phase, translations)
 
 
 def solution(mesh):

time: 55.4 us -> 52 us (0.939)
  local copies, waits for them, and re-layouts: 3.86 us -> 2.47 us
  other arithmetic: 1.3 us -> 0 us
    broadcast_in_dim x1 -> x0, local copies, waits for them, and re-layouts: 3.14 us -> none  [on_device(): return jnp.transpose(result, (1, 2, 0, 3))[:, :, None]]
    unnamed x0 -> x1, local copies, waits for them, and re-layouts: none -> 2.47 us
    another operation x1 -> x0, other arithmetic: 1.3 us -> none  [on_device(): lists = jnp.stack([partner_ids, partner_kinds, lengths])]
    another operation x1 -> x0, local copies, waits for them, and re-layouts: 0.72 us -> none  [on_device(): lists = jnp.stack([partner_ids, partner_kinds, lengths])]
where the time goes in v3:
time: 52 us; the launch traced here: 51.8 us
  Pallas kernels  49.4 us (95%)
  local copies, waits for them, and re-layouts  2.47 us (5%)
    pallas_call x1, Pallas kernels, on_device(): pl.pallas_call(functools.partial(fused_kernel, parents, span, coarse * di...  49.4 us
    unnamed x1, local copies, waits for them, and re-layouts  2.47 us

profile of v3, /device:TPU:0, one launch (start us, length us, event | category | flops | bytes accessed | tf_op | source)
XLA Modules:
  0.0 51.8 jit_solution(5071371389548486519)
XLA Ops:
  0.0 49.4 %shard_map.82 = f32[2,8,1,8,2560]{4,3,2,1,0:T(8,128)} custom-call(s32[8,128]{1,0:T(8,128)} %ids_in.1, s32[8,128]{1,0:T(8,128)} %kinds_in.1, s32[1,8]{1,0:T(1,128)} %bitcast.1, f32[2,128,2560]{2,1,0:T(8,128)} %children_ref.1, s32[4,10240]{1,0:T(4,128)} %index_in.1, f32[4,10240]{1,0:T(4,128)} %weight_in.1, f32[8,10240]{1,0:T(8,128)} %phase_in.1, ...), custom_call_target="tpu_custom_call" | custom-call | tf_op jit(solution)/shard_map/pallas_call | solution.py:467
  49.4 2.5 %copy.10 = f32[2,8,1,8,2560]{4,3,2,1,0:T(8,128)} copy(f32[2,8,1,8,2560]{4,3,2,1,0:T(8,128)} %shard_map.82) | data formatting | bytes 2621440

commit v4 on v3

--- a/solution.py
+++ b/solution.py
@@ -203,12 +203,24 @@
             held_ref.at[tile], load_sems.at[tile],
         )
 
-    @pl.loop(0, tiles)
-    def _(tile):
-        load(tile).start()
-
-    for copy in inputs:
+    per = tiles // boxes
+    early = (0, 1, 2) if chunks >= 3 else tuple(range(per))
+    late = tuple(range(3, per)) if chunks >= 3 else ()
+
+    def over_sections(offsets, act):
+        @pl.loop(0, boxes)
+        def _(section):
+            for offset in offsets:
+                act(section * per + offset)
+
+    def prepare(tile):
+        prepare_columns(held_ref, left_ref, right_ref, tile, high_ref, low_ref, parents)
+
+    over_sections(early, lambda tile: load(tile).start())
+    for copy in inputs[3:6] + inputs[:3]:
         copy.start()
+    over_sections(late, lambda tile: load(tile).start())
+    inputs[6].start()
 
     barrier = pltpu.get_barrier_semaphore()
 
@@ -219,6 +231,20 @@
     @pl.loop(1, boxes)
     def _(step):
         pl.semaphore_signal(barrier, inc=1, device_id={"box": box_at(step)}, device_id_type=mesh_type)
+
+    def clear():
+        for ref in (high_a, low_a, high_b, low_b):
+            ref[...] = jnp.zeros_like(ref)
+
+    clear()
+    over_sections(early, lambda tile: load(tile).wait())
+    if chunks >= 3:
+        over_sections((1, 2), prepare)
+    else:
+
+        @pl.loop(1, tiles)
+        def _(tile):
+            prepare(tile)
 
     pl.semaphore_wait(barrier, dirs + boxes - 2)
 
@@ -287,19 +313,13 @@
             result_ref.at[chunk, 0], dir_target(chunk, my_dir), self_sems.at[1, chunk]
         )
 
-    def clear():
-        for ref in (high_a, low_a, high_b, low_b):
-            ref[...] = jnp.zeros_like(ref)
-
-    clear()
-
-    @pl.loop(0, tiles)
-    def _(tile):
-        load(tile).wait()
-
-    @pl.loop(1, tiles)
-    def _(tile):
-        prepare_columns(held_ref, left_ref, right_ref, tile, high_ref, low_ref, parents)
+    def rest():
+        over_sections(late, lambda tile: load(tile).wait())
+        over_sections(late, prepare)
+
+        @pl.loop(1, boxes)
+        def _(section):
+            prepare(section * per)
 
     def edges():
         for copy in halos:
@@ -363,12 +383,16 @@
         def sum_tile(d, tile, buffer):
             buffer[...] = jnp.dot(counts_ref[d], sources_ref[tile], preferred_element_type=F32)
 
-        def items(step, parity):
+        def step_at(turn):
+            half = (turn + 1) // 2
+            return (dirs // 2 + jnp.where(turn % 2 == 1, half, -half) + dirs) % dirs
+
+        def items(step, following, parity):
             for tile in range(count):
                 if tile + 1 < count:
                     sum_tile(dir_at(step), tile + 1, buffers[(parity + tile + 1) % 2])
                 else:
-                    sum_tile(dir_at(step + 1), 0, buffers[(parity + tile + 1) % 2])
+                    sum_tile(dir_at(following), 0, buffers[(parity + tile + 1) % 2])
                 multiply_tile(buffers[(parity + tile) % 2], wide_ref, tile, result_ref.at[chunk, step])
 
         def send(step):
@@ -376,13 +400,13 @@
             def _():
                 dir_copy(chunk, step, my_dir).start()
 
-        sum_tile(dir_at(1), 0, summed_even)
+        sum_tile(dir_at(step_at(0)), 0, summed_even)
         if count % 2 == 0:
 
             @pl.loop(0, dirs)
             def _(turn):
-                step = (turn + 1) % dirs
-                items(step, 0)
+                step = step_at(turn)
+                items(step, step_at(turn + 1), 0)
                 send(step)
 
         else:
@@ -390,8 +414,8 @@
             @pl.loop(0, dirs // 2)
             def _(turn):
                 for half in range(2):
-                    step = (2 * turn + half + 1) % dirs
-                    items(step, half)
+                    step = step_at(2 * turn + half)
+                    items(step, step_at(2 * turn + half + 1), half)
                     send(step)
 
         own_dir_copy(chunk).start()
@@ -401,20 +425,24 @@
 
     @pl.loop(0, chunks + 1)
     def _(turn):
-        if chunks >= 3:
-            pl.when(turn == chunks - 2)(edges)
-
-        @pl.when(turn < chunks)
-        def _():
-            aggregate((turn + 1) % chunks)
-
-        @pl.when(turn == 0)
-        def _():
-            lists()
-
         @pl.when(turn > 0)
         def _():
             translate(turn % chunks)
+
+        low = jnp.where(turn == 0, 0, jnp.where(turn == 1, 1, turn + 1))
+        high = jnp.where(turn == 0, 1, jnp.minimum(turn + 2, chunks))
+
+        @pl.loop(low, high)
+        def _(order):
+            if chunks >= 3:
+                pl.when(order == chunks - 2)(edges)
+            aggregate((order + 1) % chunks)
+
+        @pl.when(turn == 0)
+        def _():
+            if chunks >= 3:
+                rest()
+            lists()
 
     for copy in halos:
         copy.wait_send()

time: 52 us -> 53.9 us (1.037)
  Pallas kernels: 49.4 us -> 51.3 us
    pallas_call x1, Pallas kernels: 49.4 us -> 51.3 us  [on_device(): pl.pallas_call(functools.partial(fused_kernel, parents, span, coarse * di...]
where the time goes in v4:
time: 53.9 us; the launch traced here: 53.8 us
  Pallas kernels  51.3 us (95%)
  local copies, waits for them, and re-layouts  2.47 us (5%)
    pallas_call x1, Pallas kernels, on_device(): pl.pallas_call(functools.partial(fused_kernel, parents, span, coarse * di...  51.3 us
    unnamed x1, local copies, waits for them, and re-layouts  2.47 us

profile of v4, /device:TPU:0, one launch (start us, length us, event | category | flops | bytes accessed | tf_op | source)
XLA Modules:
  0.0 53.8 jit_solution(4955891633500980202)
XLA Ops:
  0.0 51.3 %shard_map.82 = f32[2,8,1,8,2560]{4,3,2,1,0:T(8,128)} custom-call(s32[8,128]{1,0:T(8,128)} %ids_in.1, s32[8,128]{1,0:T(8,128)} %kinds_in.1, s32[1,8]{1,0:T(1,128)} %bitcast.1, f32[2,128,2560]{2,1,0:T(8,128)} %children_ref.1, s32[4,10240]{1,0:T(4,128)} %index_in.1, f32[4,10240]{1,0:T(4,128)} %weight_in.1, f32[8,10240]{1,0:T(8,128)} %phase_in.1, ...), custom_call_target="tpu_custom_call" | custom-call | tf_op jit(solution)/shard_map/pallas_call | solution.py:495
  51.3 2.5 %copy.10 = f32[2,8,1,8,2560]{4,3,2,1,0:T(8,128)} copy(f32[2,8,1,8,2560]{4,3,2,1,0:T(8,128)} %shard_map.82) | data formatting | bytes 2621440

commit v5 on v3

--- a/solution.py
+++ b/solution.py
@@ -106,7 +106,7 @@
         out_ref[1, :, lanes] = imag
 
 
-def count_pairs(lists_ref, kinds, sources, loose_ref, counts_ref):
+def count_pairs(lists_ref, kinds, sources, counts_ref):
     slots = lists_ref.shape[3]
     slot = lax.broadcasted_iota(jnp.int32, (1, slots), 1)
     kind = lax.broadcasted_iota(jnp.int32, (kinds, slots), 0)
@@ -121,10 +121,7 @@
             pairs = lax.dot_general(
                 kind_hot, source_hot, (((1,), (1,)), ((), ())), preferred_element_type=F32
             )
-            for part in range(loose_ref.shape[0]):
-                loose_ref[part, pl.ds(p, kinds, stride=8), :] = pairs[:, part * LANES : (part + 1) * LANES]
-        for part in range(loose_ref.shape[0]):
-            counts_ref[d, :, pl.ds(part * LANES, LANES)] = loose_ref[part].astype(BF16)
+            counts_ref[d, pl.ds(p * kinds, kinds), :] = pairs.astype(BF16)
 
 
 def load_sources(grid_ref, sources_ref):
@@ -140,35 +137,49 @@
                 sources_ref[tile, pl.ds(sources + b * parents, parents), columns] = low
 
 
-def spread_table(table_ref, column, wide_ref):
-    @pl.loop(0, table_ref.shape[1] // 8)
-    def _(group):
-        for tile in range(wide_ref.shape[0]):
-            lanes = pl.ds(pl.multiple_of(column + tile * LANES, LANES), LANES)
-            for part in range(2):
-                for k in range(8):
-                    row = table_ref[part, pl.ds(pl.multiple_of(group * 8, 8), 8), lanes][k : k + 1]
-                    wide_ref[tile, part, group * 8 + k] = jnp.broadcast_to(row, (8, LANES))
-
-
-def multiply_tile(summed_ref, wide_ref, tile, out_ref):
-    real = jnp.zeros((8, LANES), F32)
-    imag = jnp.zeros((8, LANES), F32)
-    for k in range(wide_ref.shape[2]):
-        table_real, table_imag = wide_ref[tile, 0, k], wide_ref[tile, 1, k]
-        summed_real = summed_ref[pl.ds(k * 8, 8), pl.ds(0, LANES)]
-        summed_imag = summed_ref[pl.ds(k * 8, 8), pl.ds(LANES, LANES)]
-        real = real + (table_real * summed_real - table_imag * summed_imag)
-        imag = imag + (table_real * summed_imag + table_imag * summed_real)
-    out_ref[0, :, pl.ds(tile * LANES, LANES)] = real
-    out_ref[1, :, pl.ds(tile * LANES, LANES)] = imag
+def fold(values):
+    row = lax.broadcasted_iota(jnp.int32, (8, LANES), 0)
+    lower = row < 4
+    values = [
+        jnp.where(lower, a, b) + pltpu.roll(jnp.where(lower, b, a), 4, axis=0)
+        for a, b in zip(values[:4], values[4:])
+    ]
+    for reach in (2, 1):
+        lower = row % (2 * reach) < reach
+        values = [
+            jnp.where(lower, a + pltpu.roll(a, 8 - reach, axis=0), b + pltpu.roll(b, reach, axis=0))
+            for a, b in zip(values[:reach], values[reach:])
+        ]
+    return values[0]
+
+
+def multiply_tile(summed_ref, table_ref, column, tile, out_ref):
+    kinds = table_ref.shape[1]
+    lanes = pl.ds(pl.multiple_of(column + tile * LANES, LANES), LANES)
+    groups = range(0, kinds, 8)
+    table_real = [table_ref[0, pl.ds(k, 8), lanes] for k in groups]
+    table_imag = [table_ref[1, pl.ds(k, 8), lanes] for k in groups]
+    reals, imags = [], []
+    for p in range(8):
+        real, imag = None, None
+        for k, tr, ti in zip(groups, table_real, table_imag):
+            summed_real = summed_ref[pl.ds(p * kinds + k, 8), pl.ds(0, LANES)]
+            summed_imag = summed_ref[pl.ds(p * kinds + k, 8), pl.ds(LANES, LANES)]
+            add_real = tr * summed_real - ti * summed_imag
+            add_imag = tr * summed_imag + ti * summed_real
+            real = add_real if real is None else real + add_real
+            imag = add_imag if imag is None else imag + add_imag
+        reals.append(real)
+        imags.append(imag)
+    out_ref[0, :, pl.ds(tile * LANES, LANES)] = fold(reals)
+    out_ref[1, :, pl.ds(tile * LANES, LANES)] = fold(imags)
 
 
 def fused_kernel(
     parents, span, total, ids_in, kinds_in, lengths_in, children_ref, index_in, weight_in, phase_in, table_in, out_ref,
     held_ref, left_ref, right_ref, index_ref, weight_ref, phase_ref, table_ref, lists_ref, spare_ref,
     high_ref, low_ref, high_a, low_a, fine_a, high_b, low_b, fine_b, outgoing_ref, grid_ref,
-    loose_ref, counts_ref, sources_ref, wide_ref, summed_even, summed_odd, result_ref, landing_ref,
+    counts_ref, sources_ref, summed_even, summed_odd, result_ref, landing_ref,
     load_sems, input_sems, self_sems, halo_send, halo_recv, list_send, list_recv,
     box_send, box_recv, dir_send, dir_recv, place_sems,
 ):
@@ -312,7 +323,7 @@
         def _(step):
             list_copy(step, dir_at(-step)).wait_recv()
 
-        count_pairs(lists_ref, kinds, sources_ref.shape[1] // 2, loose_ref, counts_ref)
+        count_pairs(lists_ref, kinds, sources_ref.shape[1] // 2, counts_ref)
         inputs[6].wait()
 
     for copy in inputs[:3]:
@@ -349,7 +360,6 @@
         own_box_copy(chunk).start()
 
     def translate(chunk):
-        spread_table(table_ref, chunk * block, wide_ref)
         own_box_copy(chunk).wait()
 
         @pl.loop(1, boxes)
@@ -369,7 +379,9 @@
                     sum_tile(dir_at(step), tile + 1, buffers[(parity + tile + 1) % 2])
                 else:
                     sum_tile(dir_at(step + 1), 0, buffers[(parity + tile + 1) % 2])
-                multiply_tile(buffers[(parity + tile) % 2], wide_ref, tile, result_ref.at[chunk, step])
+                multiply_tile(
+                    buffers[(parity + tile) % 2], table_ref, chunk * block, tile, result_ref.at[chunk, step]
+                )
 
         def send(step):
             @pl.when(step > 0)
@@ -489,10 +501,8 @@
             vmem((2 * rows, block), F32),
             vmem((chunks, boxes, 2, parents, block), F32),
             vmem((chunks, boxes, 2, parents, block), F32),
-            vmem((2 * sources // LANES, kinds * 8, LANES), F32),
             vmem((dirs, kinds * 8, 2 * sources), BF16),
             vmem((block // LANES, 2 * sources, 2 * LANES), BF16),
-            vmem((block // LANES, 2, kinds, 8, LANES), F32),
             vmem((kinds * 8, 2 * LANES), F32),
             vmem((kinds * 8, 2 * LANES), F32),
             vmem((chunks, dirs, 2, 8, block), F32),

time: 52 us -> 51.6 us (level)
  no operation moved by 1% of the time
where the time goes in v5:
time: 51.6 us; the launch traced here: 51.4 us
  Pallas kernels  48.9 us (95%)
  local copies, waits for them, and re-layouts  2.47 us (5%)
    pallas_call x1, Pallas kernels, on_device(): pl.pallas_call(functools.partial(fused_kernel, parents, span, coarse * di...  48.9 us
    unnamed x1, local copies, waits for them, and re-layouts  2.47 us

profile of v5, /device:TPU:0, one launch (start us, length us, event | category | flops | bytes accessed | tf_op | source)
XLA Modules:
  0.0 51.4 jit_solution(10013303235920537183)
XLA Ops:
  0.0 48.9 %shard_map.82 = f32[2,8,1,8,2560]{4,3,2,1,0:T(8,128)} custom-call(s32[8,128]{1,0:T(8,128)} %ids_in.1, s32[8,128]{1,0:T(8,128)} %kinds_in.1, s32[1,8]{1,0:T(1,128)} %bitcast.1, f32[2,128,2560]{2,1,0:T(8,128)} %children_ref.1, s32[4,10240]{1,0:T(4,128)} %index_in.1, f32[4,10240]{1,0:T(4,128)} %weight_in.1, f32[8,10240]{1,0:T(8,128)} %phase_in.1, ...), custom_call_target="tpu_custom_call" | custom-call | tf_op jit(solution)/shard_map/pallas_call | solution.py:479
  48.9 2.5 %copy.10 = f32[2,8,1,8,2560]{4,3,2,1,0:T(8,128)} copy(f32[2,8,1,8,2560]{4,3,2,1,0:T(8,128)} %shard_map.82) | data formatting | bytes 2621440

commit v6 on v5

--- a/solution.py
+++ b/solution.py
@@ -214,12 +214,24 @@
             held_ref.at[tile], load_sems.at[tile],
         )
 
-    @pl.loop(0, tiles)
-    def _(tile):
-        load(tile).start()
-
-    for copy in inputs:
+    per = tiles // boxes
+    early = (0, 1, 2) if chunks >= 3 else tuple(range(per))
+    late = tuple(range(3, per)) if chunks >= 3 else ()
+
+    def over_sections(offsets, act):
+        @pl.loop(0, boxes)
+        def _(section):
+            for offset in offsets:
+                act(section * per + offset)
+
+    def prepare(tile):
+        prepare_columns(held_ref, left_ref, right_ref, tile, high_ref, low_ref, parents)
+
+    over_sections(early, lambda tile: load(tile).start())
+    for copy in inputs[3:6] + inputs[:3]:
         copy.start()
+    over_sections(late, lambda tile: load(tile).start())
+    inputs[6].start()
 
     barrier = pltpu.get_barrier_semaphore()
 
@@ -230,6 +242,20 @@
     @pl.loop(1, boxes)
     def _(step):
         pl.semaphore_signal(barrier, inc=1, device_id={"box": box_at(step)}, device_id_type=mesh_type)
+
+    def clear():
+        for ref in (high_a, low_a, high_b, low_b):
+            ref[...] = jnp.zeros_like(ref)
+
+    clear()
+    over_sections(early, lambda tile: load(tile).wait())
+    if chunks >= 3:
+        over_sections((1, 2), prepare)
+    else:
+
+        @pl.loop(1, tiles)
+        def _(tile):
+            prepare(tile)
 
     pl.semaphore_wait(barrier, dirs + boxes - 2)
 
@@ -298,19 +324,13 @@
             result_ref.at[chunk, 0], dir_target(chunk, my_dir), self_sems.at[1, chunk]
         )
 
-    def clear():
-        for ref in (high_a, low_a, high_b, low_b):
-            ref[...] = jnp.zeros_like(ref)
-
-    clear()
-
-    @pl.loop(0, tiles)
-    def _(tile):
-        load(tile).wait()
-
-    @pl.loop(1, tiles)
-    def _(tile):
-        prepare_columns(held_ref, left_ref, right_ref, tile, high_ref, low_ref, parents)
+    def rest():
+        over_sections(late, lambda tile: load(tile).wait())
+        over_sections(late, prepare)
+
+        @pl.loop(1, boxes)
+        def _(section):
+            prepare(section * per)
 
     def edges():
         for copy in halos:
@@ -422,6 +442,8 @@
 
         @pl.when(turn == 0)
         def _():
+            if chunks >= 3:
+                rest()
             lists()
 
         @pl.when(turn > 0)

time: 51.6 us -> 51.6 us (level)
  no operation moved by 1% of the time
where the time goes in v6:
time: 51.6 us; the launch traced here: 51.4 us
  Pallas kernels  48.9 us (95%)
  local copies, waits for them, and re-layouts  2.47 us (5%)
    pallas_call x1, Pallas kernels, on_device(): pl.pallas_call(functools.partial(fused_kernel, parents, span, coarse * di...  48.9 us
    unnamed x1, local copies, waits for them, and re-layouts  2.47 us

profile of v6, /device:TPU:0, one launch (start us, length us, event | category | flops | bytes accessed | tf_op | source)
XLA Modules:
  0.0 51.4 jit_solution(3724639949626104688)
XLA Ops:
  0.0 48.9 %shard_map.82 = f32[2,8,1,8,2560]{4,3,2,1,0:T(8,128)} custom-call(s32[8,128]{1,0:T(8,128)} %ids_in.1, s32[8,128]{1,0:T(8,128)} %kinds_in.1, s32[1,8]{1,0:T(1,128)} %bitcast.1, f32[2,128,2560]{2,1,0:T(8,128)} %children_ref.1, s32[4,10240]{1,0:T(4,128)} %index_in.1, f32[4,10240]{1,0:T(4,128)} %weight_in.1, f32[8,10240]{1,0:T(8,128)} %phase_in.1, ...), custom_call_target="tpu_custom_call" | custom-call | tf_op jit(solution)/shard_map/pallas_call | solution.py:501
  48.9 2.5 %copy.10 = f32[2,8,1,8,2560]{4,3,2,1,0:T(8,128)} copy(f32[2,8,1,8,2560]{4,3,2,1,0:T(8,128)} %shard_map.82) | data formatting | bytes 2621440

commit v7 on v6

--- a/solution.py
+++ b/solution.py
@@ -393,12 +393,16 @@
         def sum_tile(d, tile, buffer):
             buffer[...] = jnp.dot(counts_ref[d], sources_ref[tile], preferred_element_type=F32)
 
-        def items(step, parity):
+        def step_at(turn):
+            half = (turn + 1) // 2
+            return (dirs // 2 + jnp.where(turn % 2 == 1, half, -half) + dirs) % dirs
+
+        def items(step, following, parity):
             for tile in range(count):
                 if tile + 1 < count:
                     sum_tile(dir_at(step), tile + 1, buffers[(parity + tile + 1) % 2])
                 else:
-                    sum_tile(dir_at(step + 1), 0, buffers[(parity + tile + 1) % 2])
+                    sum_tile(dir_at(following), 0, buffers[(parity + tile + 1) % 2])
                 multiply_tile(
                     buffers[(parity + tile) % 2], table_ref, chunk * block, tile, result_ref.at[chunk, step]
                 )
@@ -408,13 +412,13 @@
             def _():
                 dir_copy(chunk, step, my_dir).start()
 
-        sum_tile(dir_at(1), 0, summed_even)
+        sum_tile(dir_at(step_at(0)), 0, summed_even)
         if count % 2 == 0:
 
             @pl.loop(0, dirs)
             def _(turn):
-                step = (turn + 1) % dirs
-                items(step, 0)
+                step = step_at(turn)
+                items(step, step_at(turn + 1), 0)
                 send(step)
 
         else:
@@ -422,8 +426,8 @@
             @pl.loop(0, dirs // 2)
             def _(turn):
                 for half in range(2):
-                    step = (2 * turn + half + 1) % dirs
-                    items(step, half)
+                    step = step_at(2 * turn + half)
+                    items(step, step_at(2 * turn + half + 1), half)
                     send(step)
 
         own_dir_copy(chunk).start()

time: 51.6 us -> 51.6 us (level)
  no operation moved by 1% of the time
where the time goes in v7:
time: 51.6 us; the launch traced here: 51.4 us
  Pallas kernels  49 us (95%)
  local copies, waits for them, and re-layouts  2.47 us (5%)
    pallas_call x1, Pallas kernels, on_device(): pl.pallas_call(functools.partial(fused_kernel, parents, span, coarse * di...  49 us
    unnamed x1, local copies, waits for them, and re-layouts  2.47 us

profile of v7, /device:TPU:0, one launch (start us, length us, event | category | flops | bytes accessed | tf_op | source)
XLA Modules:
  0.0 51.4 jit_solution(9780394713644507227)
XLA Ops:
  0.0 49.0 %shard_map.82 = f32[2,8,1,8,2560]{4,3,2,1,0:T(8,128)} custom-call(s32[8,128]{1,0:T(8,128)} %ids_in.1, s32[8,128]{1,0:T(8,128)} %kinds_in.1, s32[1,8]{1,0:T(1,128)} %bitcast.1, f32[2,128,2560]{2,1,0:T(8,128)} %children_ref.1, s32[4,10240]{1,0:T(4,128)} %index_in.1, f32[4,10240]{1,0:T(4,128)} %weight_in.1, f32[8,10240]{1,0:T(8,128)} %phase_in.1, ...), custom_call_target="tpu_custom_call" | custom-call | tf_op jit(solution)/shard_map/pallas_call | solution.py:505
  49.0 2.5 %copy.10 = f32[2,8,1,8,2560]{4,3,2,1,0:T(8,128)} copy(f32[2,8,1,8,2560]{4,3,2,1,0:T(8,128)} %shard_map.82) | data formatting | bytes 2621440
